TPU v7x, 32 devices: a whole 2x2x4 slice. The times are simulated.
32 devices in a mesh: row: 8 (over z, x), vec: 4 (over y, core).
Axes of the slice: x: 2, y: 2, z: 4, core: 2. Of those that a mesh axis runs over, the one named last changes fastest.
Arguments:
- vectors: float32 [16384, 1024], P('row', 'vec'), may hold values from -8 to 8
- hamiltonian: float32 [128, 12, 128, 128], P('row'), may hold values from -0.15 to 0.15, as said below
- column_blocks: int32 [128, 12], P('row'), may hold values from 0 to 127, as said below
- live_counts: int32 [128], P('row'), may hold values from 3 to 12
- lower_bound: float32 [1], replicated, may hold values from -0.85 to -0.65
- upper_bound: float32 [1], replicated, may hold values from 1.05 to 1.3
Outputs:
- filtered: float32 [16384, 1024], P('row', 'vec')
Inputs may be any that keep to these rules, and one draw needn't show every extreme that they name: column_blocks[i, 0] = i, and every entry lies within 16 block rows of its row i, cyclically modulo 128; the distances 16 and -16 both occur. `hamiltonian`: H is symmetric: for every used slot of block row i that names column block j there is a used slot of block row j that names i and holds the transpose of its block, and slot 0 of every block row holds a symmetric block.
All inputs are finite; a program needn't handle non-finite values.
Results may differ from a plain program's by a relative error of at most 0.0003.
Values sent between devices are 32-bit elements; how exact they have to be, the bound alone decides.
A program may use at most 128 MiB of HBM per device.

v0:
```python
import math

import jax
import jax.numpy as jnp
from jax import lax
from jax.sharding import PartitionSpec as P

NV = 1024
NS_ITERS = 3


def with_halo(cells, sides, width):
    for axis, dim in sides:
        count = lax.axis_size(axis)
        head = lax.slice_in_dim(cells, 0, width, axis=dim)
        tail = lax.slice_in_dim(cells, cells.shape[dim] - width, cells.shape[dim], axis=dim)
        cells = jnp.concatenate(
            [
                lax.ppermute(tail, axis, [(i, (i + 1) % count) for i in range(count)]),
                cells,
                lax.ppermute(head, axis, [((i + 1) % count, i) for i in range(count)]),
            ],
            axis=dim,
        )
    return cells


def on_device(vectors, hamiltonian, column_blocks, live_counts, lower_bound, upper_bound):
    rows_dev, panel_cols = vectors.shape
    block_rows, slot_count, block_size, unused_size = hamiltonian.shape
    row_count = lax.axis_size("row")
    first_row = lax.axis_index("row") * block_rows
    local_cols = (column_blocks - first_row + block_rows) % (block_rows * row_count)

    def apply_field(operand):
        widened = with_halo(operand, (("row", 0),), block_rows * block_size)
        widened_blocks = widened.reshape(3 * block_rows, block_size, panel_cols)
        picked = jnp.take(widened_blocks, local_cols, axis=0)
        live_mask = (
            jnp.arange(slot_count, dtype=jnp.int32)[None, :] < live_counts[:, None]
        ).astype(jnp.float32)
        summed = jnp.einsum(
            "rkij,rkjc->ric",
            hamiltonian,
            picked * live_mask[:, :, None, None],
            precision=lax.Precision.HIGHEST,
            preferred_element_type=jnp.float32,
        )
        return summed.reshape(rows_dev, panel_cols)

    centre = (upper_bound[0] + lower_bound[0]) / 2
    radius = (upper_bound[0] - lower_bound[0]) / 2
    first = (apply_field(vectors) - centre * vectors) / radius
    second = 2 * (apply_field(first) - centre * first) / radius - vectors
    energy = lax.psum(jnp.sum(second * second), ("row", "vec"))
    current = second * jnp.sqrt(NV / (4 * (energy + 1e-06)))
    for iteration in range(NS_ITERS):
        full_rows = lax.all_gather(current, "vec", axis=1, tiled=True)
        local_gram = jnp.einsum(
            "rc,rd->cd",
            full_rows,
            current,
            precision=lax.Precision.HIGHEST,
            preferred_element_type=jnp.float32,
        )
        gram_part = lax.psum(local_gram, "row")
        current = 1.5 * current - 0.5 * jnp.dot(
            full_rows,
            gram_part,
            precision=lax.Precision.HIGHEST,
            preferred_element_type=jnp.float32,
        )
    total_rows = rows_dev * row_count
    return current * math.sqrt(total_rows)


def solution(mesh):
    placed = (P("row", "vec"), P("row", None, None, None), P("row", None), P("row"), P(), P())
    return jax.shard_map(
        on_device, mesh=mesh, in_specs=placed, out_specs=P("row", "vec"), check_vma=False
    )
```

profile of v0, /device:TPU:23, one launch (start us, length us, event | category | flops | bytes accessed | tf_op | source)
XLA Modules:
  0.0 820.0 jit_solution(17545777189886878566)
XLA Ops:
  6.5 0.0 all-gather.4.cloned.1.call-start
  6.5 0.3 collective-permute-start.1
  6.8 2.1 collective-permute-start
  10.2 0.8 compare_and_fusion
  11.0 0.1 reshape.69
  11.1 85.3 %collective-permute-done.1 = f32[2048,256]{1,0:T(8,128)S(1)} collective-permute-done((f32[2048,256]{1,0:T(8,128)}, f32[2048,256]{1,0:T(8,128)S(1)}, u32[]{:S(2)}, u32[]{:S(2)}) %collective-permute-start.1) | collective-permute-done | bytes 2097184 | tf_op jit(solution)/shard_map/ppermute | solution.py:21
  96.3 2.6 collective-permute-done
  98.9 5.3 pad_maximum_fusion
  104.2 15.2 %gather_fusion = f32[192,128,256]{2,1,0:T(8,128)} fusion(f32[48,128,256]{2,1,0:T(8,128)} %bitcast.49, s32[1024]{0:T(1024)S(1)} %pad_clamp_fusion), kind=kCustom, calls=%fused_computation.clone | custom fusion | bytes 50332416 | tf_op jit(solution)/shard_map/jit(_take)/gather | solution.py:38
  119.4 21.3 %fusion.1 = f32[16,256,128,1]{1,2,3,0:T(8,128)S(1)} fusion(f32[16,12,128,128]{3,2,1,0:T(8,128)} %param.9, f32[16,12,128,256]{3,2,1,0:T(8,128)} %bitcast.47, f32[16,12]{1,0:T(8,128)S(1)} %get-tuple-element.10, pred[16,12]{1,0:T(8,128)(4,1)S(1)} %get-tuple-element.8), kind=kOutput, calls=%fused_computation.5 | convolution fusion | flops 9676259328 | bytes 39846848 | tf_op jit(solution)/shard_map/rkij,rkjc->ric/dot_general | solution.py:42
  140.7 2.1 fusion.15
  142.8 0.1 collective-permute-start.3
  142.8 2.8 collective-permute-start.2
  145.6 86.0 %collective-permute-done.3 = f32[2048,256]{1,0:T(8,128)S(1)} collective-permute-done((f32[2048,256]{1,0:T(8,128)S(1)}, f32[2048,256]{1,0:T(8,128)S(1)}, u32[]{:S(2)}, u32[]{:S(2)}) %collective-permute-start.3) | collective-permute-done | bytes 2097184 | tf_op jit(solution)/shard_map/ppermute | solution.py:21
  231.6 3.8 collective-permute-done.2
  235.4 3.1 pad_maximum_fusion.1
  238.5 15.2 %gather_fusion.1 = f32[192,128,256]{2,1,0:T(8,128)} fusion(f32[48,128,256]{2,1,0:T(8,128)} %bitcast.48, s32[1024]{0:T(1024)S(1)} %pad_clamp_fusion), kind=kCustom, calls=%fused_computation.1.clone | custom fusion | bytes 50332416 | tf_op jit(solution)/shard_map/jit(_take)/gather | solution.py:38
  253.7 22.1 %fusion = f32[16,256,128,1]{1,2,3,0:T(8,128)} fusion(f32[16,12,128,128]{3,2,1,0:T(8,128)} %param.9, f32[16,12,128,256]{3,2,1,0:T(8,128)} %bitcast.46, f32[16,12]{1,0:T(8,128)S(1)} %get-tuple-element.10, pred[16,12]{1,0:T(8,128)(4,1)S(1)} %get-tuple-element.8), kind=kOutput, calls=%fused_computation.3 | convolution fusion | flops 9676259328 | bytes 39846848 | tf_op jit(solution)/shard_map/rkij,rkjc->ric/dot_general | solution.py:42
  275.8 4.9 multiply_reduce_fusion
  280.6 39.6 %psum.28 = f32[]{:T(128)} all-reduce(f32[]{:T(128)} %get-tuple-element.6), channel_id=1, replica_groups=mesh['row'=8,'vec'=4] {'row','vec'}, use_global_device_ids=true, to_apply=%region_1.3 | all-reduce | flops 1 | bytes 8 | tf_op jit(solution)/shard_map/psum | solution.py:55
  321.0 3.0 broadcast_multiply_fusion
  324.1 0.0 copy-start.2
  324.1 0.0 all-gather.4.cloned.1.call-update
  324.1 0.2 all-reduce.4.cloned.1.call-start
  324.3 58.6 %all-gather.4.cloned.1.call-done = f32[2048,1024]{1,0:T(8,128)} async-done(((f32[2048,256]{1,0:T(8,128)}), f32[2048,1024]{1,0:T(8,128)}) %all-gather.4.cloned.1.call-update) | async-done | bytes 8388624 | tf_op jit(solution)/shard_map/all_gather | solution.py:58
  382.9 0.0 copy-done.2
  382.9 16.3 %fusion.21 = f32[1024,256]{1,0:T(8,128)} fusion(f32[2048,1024]{1,0:T(8,128)} %all-gather.4.cloned.1.call-done, f32[2048,256]{1,0:T(8,128)S(1)} %copy-done.2), kind=kOutput, calls=%fused_computation.40 | convolution fusion | flops 6442450944 | bytes 11534336 | tf_op jit(solution)/shard_map/rc,rd->cd/dot_general | solution.py:59
  399.3 0.0 all-reduce.4.cloned.1.call-update
  399.3 0.0 all-gather.6.cloned.1.call-start
  399.3 77.3 %all-reduce.4.cloned.1.call-done = f32[1024,256]{1,0:T(8,128)} async-done(((f32[1024,256]{1,0:T(8,128)}), f32[1024,256]{1,0:T(8,128)}) %all-reduce.4.cloned.1.call-update) | async-done | bytes 1048592 | tf_op jit(solution)/shard_map/psum | solution.py:66
  476.7 10.3 %fusion.8 = f32[2048,256]{1,0:T(8,128)} fusion(f32[2048,1024]{1,0:T(8,128)} %all-gather.4.cloned.1.call-done, f32[1024,256]{1,0:T(8,128)} %all-reduce.4.cloned.1.call-done, f32[2048,256]{1,0:T(8,128)S(1)} %copy-done.2), kind=kOutput, calls=%fused_computation.17 | convolution fusion | flops 6444023808 | bytes 13631488 | tf_op jit(solution)/shard_map/dot_general | solution.py:67
  487.0 0.0 all-gather.6.cloned.1.call-update
  487.0 0.3 all-reduce.6.cloned.1.call-start
  487.3 58.7 %all-gather.6.cloned.1.call-done = f32[2048,1024]{1,0:T(8,128)} async-done(((f32[2048,256]{1,0:T(8,128)}), f32[2048,1024]{1,0:T(8,128)}) %all-gather.6.cloned.1.call-update) | async-done | bytes 8388624 | tf_op jit(solution)/shard_map/all_gather | solution.py:58
  546.0 0.0 copy-done
  546.0 16.3 %fusion.22 = f32[1024,256]{1,0:T(8,128)} fusion(f32[2048,1024]{1,0:T(8,128)} %all-gather.6.cloned.1.call-done, f32[2048,256]{1,0:T(8,128)S(1)} %copy-done), kind=kOutput, calls=%fused_computation.41 | convolution fusion | flops 6442450944 | bytes 11534336 | tf_op jit(solution)/shard_map/rc,rd->cd/dot_general | solution.py:59
  562.3 0.0 all-reduce.6.cloned.1.call-update
  562.3 0.0 all-gather.8.cloned.1.call-start
  562.3 77.2 %all-reduce.6.cloned.1.call-done = f32[1024,256]{1,0:T(8,128)} async-done(((f32[1024,256]{1,0:T(8,128)}), f32[1024,256]{1,0:T(8,128)}) %all-reduce.6.cloned.1.call-update) | async-done | bytes 1048592 | tf_op jit(solution)/shard_map/psum | solution.py:66
  639.5 10.3 %fusion.9 = f32[2048,256]{1,0:T(8,128)} fusion(f32[2048,1024]{1,0:T(8,128)} %all-gather.6.cloned.1.call-done, f32[1024,256]{1,0:T(8,128)} %all-reduce.6.cloned.1.call-done, f32[2048,256]{1,0:T(8,128)S(1)} %copy-done), kind=kOutput, calls=%fused_computation.18 | convolution fusion | flops 6444023808 | bytes 13631488 | tf_op jit(solution)/shard_map/dot_general | solution.py:67
  649.8 0.0 all-gather.8.cloned.1.call-update
  649.9 0.3 all-reduce.8.cloned.1.call-start
  650.2 58.6 %all-gather.8.cloned.1.call-done = f32[2048,1024]{1,0:T(8,128)} async-done(((f32[2048,256]{1,0:T(8,128)}), f32[2048,1024]{1,0:T(8,128)}) %all-gather.8.cloned.1.call-update) | async-done | bytes 8388624 | tf_op jit(solution)/shard_map/all_gather | solution.py:58
  708.8 0.0 copy-done.1
  708.8 16.3 %fusion.23 = f32[1024,256]{1,0:T(8,128)} fusion(f32[2048,1024]{1,0:T(8,128)} %all-gather.8.cloned.1.call-done, f32[2048,256]{1,0:T(8,128)S(1)} %copy-done.1), kind=kOutput, calls=%fused_computation.42 | convolution fusion | flops 6442450944 | bytes 11534336 | tf_op jit(solution)/shard_map/rc,rd->cd/dot_general | solution.py:59
  725.1 0.0 all-reduce.8.cloned.1.call-update
  725.1 77.3 %all-reduce.8.cloned.1.call-done = f32[1024,256]{1,0:T(8,128)} async-done(((f32[1024,256]{1,0:T(8,128)}), f32[1024,256]{1,0:T(8,128)}) %all-reduce.8.cloned.1.call-update) | async-done | bytes 1048592 | tf_op jit(solution)/shard_map/psum | solution.py:66
  802.4 10.3 %fusion.11 = f32[2048,256]{1,0:T(8,128)} fusion(f32[2048,1024]{1,0:T(8,128)} %all-gather.8.cloned.1.call-done, f32[1024,256]{1,0:T(8,128)} %all-reduce.8.cloned.1.call-done, f32[2048,256]{1,0:T(8,128)S(1)} %copy-done.1), kind=kOutput, calls=%fused_computation.20 | convolution fusion | flops 6444548096 | bytes 13631488 | tf_op jit(solution)/shard_map/dot_general | solution.py:67
  (3 shorter events, 0.0 us)
Async XLA Ops:
  6.5 376.4 %all-gather.4.cloned.1.call-start = ((), (), s32[]{:S(2)}) async-start(), calls=%async_computation | async-start | bytes 10485760 | tf_op jit(solution)/shard_map/all_gather | solution.py:58
  6.5 89.8 %collective-permute-start.1 = (f32[2048,256]{1,0:T(8,128)}, f32[2048,256]{1,0:T(8,128)S(1)}, u32[]{:S(2)}, u32[]{:S(2)}) collective-permute-start(f32[2048,256]{1,0:T(8,128)} %param.8), channel_id=1, source_target_pairs={{4,0},{8,4},{12,8},{16,12},{20,16},{24,20},{28,24},{0,28},{5,1},{9... | collective-permute-start | bytes 6291464 | tf_op jit(solution)/shard_map/ppermute | solution.py:21
  6.8 92.1 %collective-permute-start = (f32[2048,256]{1,0:T(8,128)}, f32[2048,256]{1,0:T(8,128)}, u32[]{:S(2)}, u32[]{:S(2)}) collective-permute-start(f32[2048,256]{1,0:T(8,128)} %param.8), channel_id=1, source_target_pairs={{0,4},{4,8},{8,12},{12,16},{16,20},{20,24},{24,28},{28,0},{1,5},{5... | collective-permute-start | bytes 6291464 | tf_op jit(solution)/shard_map/ppermute | solution.py:19
  142.8 88.9 %collective-permute-start.3 = (f32[2048,256]{1,0:T(8,128)S(1)}, f32[2048,256]{1,0:T(8,128)S(1)}, u32[]{:S(2)}, u32[]{:S(2)}) collective-permute-start(f32[2048,256]{1,0:T(8,128)S(1)} %fusion.15), channel_id=1, source_target_pairs={{4,0},{8,4},{12,8},{16,12},{20,16},{24,20},{28,24},{0,28},{5,1},{9... | collective-permute-start | bytes 6291464 | tf_op jit(solution)/shard_map/ppermute | solution.py:21
  142.8 92.6 %collective-permute-start.2 = (f32[2048,256]{1,0:T(8,128)S(1)}, f32[2048,256]{1,0:T(8,128)S(1)}, u32[]{:S(2)}, u32[]{:S(2)}) collective-permute-start(f32[2048,256]{1,0:T(8,128)S(1)} %fusion.15), channel_id=1, source_target_pairs={{0,4},{4,8},{8,12},{12,16},{16,20},{20,24},{24,28},{28,0},{1,5},{5... | collective-permute-start | bytes 6291464 | tf_op jit(solution)/shard_map/ppermute | solution.py:19
  324.1 58.9 %copy-start.2 = (f32[2048,256]{1,0:T(8,128)S(1)}, f32[2048,256]{1,0:T(8,128)}, u32[]{:S(2)}) copy-start(f32[2048,256]{1,0:T(8,128)} %broadcast_multiply_fusion) | copy-start | bytes 6291460
  324.1 152.6 %all-reduce.4.cloned.1.call-start = ((), (), s32[]{:S(2)}) async-start(), calls=%async_computation.1 | async-start | bytes 2097152 | tf_op jit(solution)/shard_map/psum | solution.py:66
  399.3 146.7 %all-gather.6.cloned.1.call-start = ((), (), s32[]{:S(2)}) async-start(), calls=%async_computation.2 | async-start | bytes 10485760 | tf_op jit(solution)/shard_map/all_gather | solution.py:58
  487.0 59.0 %copy-start = (f32[2048,256]{1,0:T(8,128)S(1)}, f32[2048,256]{1,0:T(8,128)}, u32[]{:S(2)}) copy-start(f32[2048,256]{1,0:T(8,128)} %fusion.8) | copy-start | bytes 6291460
  487.0 152.5 %all-reduce.6.cloned.1.call-start = ((), (), s32[]{:S(2)}) async-start(), calls=%async_computation.3 | async-start | bytes 2097152 | tf_op jit(solution)/shard_map/psum | solution.py:66
  562.3 146.5 %all-gather.8.cloned.1.call-start = ((), (), s32[]{:S(2)}) async-start(), calls=%async_computation.4 | async-start | bytes 10485760 | tf_op jit(solution)/shard_map/all_gather | solution.py:58
  649.8 59.0 %copy-start.1 = (f32[2048,256]{1,0:T(8,128)S(1)}, f32[2048,256]{1,0:T(8,128)}, u32[]{:S(2)}) copy-start(f32[2048,256]{1,0:T(8,128)} %fusion.9) | copy-start | bytes 6291460
  649.9 152.5 %all-reduce.8.cloned.1.call-start = ((), (), s32[]{:S(2)}) async-start(), calls=%async_computation.5 | async-start | bytes 2097152 | tf_op jit(solution)/shard_map/psum | solution.py:66
Sparse Core Ops, SparseCore 0:
  324.2 58.6 all-gather.3
  399.4 77.2 all-reduce.3
  487.1 58.7 all-gather.5
  562.4 77.0 all-reduce.5
  650.0 58.7 all-gather.7
  725.3 77.0 all-reduce.7
where the time goes:
time: 829 us; the launch traced here: 820 us
  waiting for transfers between devices  585 us (71%)
  matrix products  123 us (15%)
  blocking collectives  39.6 us (5%)
  local copies, waits for them, and re-layouts  30.4 us (4%)
  other arithmetic  19.2 us (2%)
  between operations  16 us (2%)
    psum x3, waiting for transfers between devices, on_device(): gram_part = lax.psum(local_gram, 'row')  232 us
    all_gather x3, waiting for transfers between devices, on_device(): full_rows = lax.all_gather(current, 'vec', axis=1, tiled=True)  176 us
    ppermute x2, waiting for transfers between devices, with_halo(): lax.ppermute(head, axis, [((i + 1) % count, i) for i in range(count)])  171 us
    dot_general x3, matrix products, on_device(): jnp.einsum('rc,rd->cd', full_rows, current, precision=lax.Precision.HIGHE...  49 us
    dot_general x2, matrix products, apply_field(): jnp.einsum('rkij,rkjc->ric', hamiltonian, picked * live_mask[:, :, None,...  43.4 us
    psum x1, blocking collectives, on_device(): energy = lax.psum(jnp.sum(second * second), ('row', 'vec'))  39.6 us
    dot_general x3, matrix products, on_device(): jnp.dot(full_rows, gram_part, precision=lax.Precision.HIGHEST, preferred_...  30.9 us
    gather x2, local copies, waits for them, and re-layouts, apply_field(): picked = jnp.take(widened_blocks, local_cols, axis=0)  30.3 us
  transfers between devices with their start and end apart: 10, of which 10 were waited for; matrix products, arithmetic and copies ran while one was open for 0% of the time, Pallas kernels for 0%

commit v1 on v0

v1 whole, which is shorter than its diff:
```python
import functools
import math

import jax
import jax.numpy as jnp
from jax import lax
from jax.experimental import pallas as pl
from jax.experimental.pallas import tpu as pltpu
from jax.sharding import PartitionSpec as P

NS_ITERS = 3
PIECES = 4


def split(x):
    hi = x.astype(jnp.bfloat16)
    return hi, (x - hi.astype(jnp.float32)).astype(jnp.bfloat16)


def dot(a, b):
    return jnp.dot(a, b, preferred_element_type=jnp.float32)


def field_kernel(has_prev, pos_ref, live_ref, coef_ref, own_ref, near_ref, far_ref, ham_ref, *rest):
    if has_prev:
        prev_ref, out_ref, hi_ref, lo_ref = rest
    else:
        out_ref, hi_ref, lo_ref = rest
    i = pl.program_id(0)
    rows = own_ref.shape[0]
    slots, size = ham_ref.shape[1], ham_ref.shape[2]

    @pl.when(i == 0)
    def _():
        for part, ref in enumerate((own_ref, near_ref, far_ref)):
            @pl.loop(0, rows // size)
            def _(b):
                hi, lo = split(ref[pl.ds(pl.multiple_of(b * size, size), size), :])
                at = pl.multiple_of(part * rows + b * size, size)
                hi_ref[pl.ds(at, size), :] = hi
                lo_ref[pl.ds(at, size), :] = lo

    live = live_ref[i]
    acc_h = None
    for k in range(0, slots, 2):
        mats = [jnp.where(s < live, ham_ref[0, s], 0.0) for s in range(k, min(k + 2, slots))]
        spots = [pl.ds(pl.multiple_of(pos_ref[i, s] * size, size), size) for s in range(k, min(k + 2, slots))]
        mhi, mlo = split(jnp.concatenate(mats, axis=1))
        vhi = jnp.concatenate([hi_ref[s, :] for s in spots], axis=0)
        vlo = jnp.concatenate([lo_ref[s, :] for s in spots], axis=0)
        both = dot(jnp.concatenate([mhi, mlo], axis=0), vhi)
        term = both[:size] + both[size:] + dot(mhi, vlo)
        acc_h = term if acc_h is None else acc_h + term
    mine = pl.ds(pl.multiple_of(i * size, size), size)
    out = (acc_h - coef_ref[0] * own_ref[mine, :]) / coef_ref[1]
    if has_prev:
        out = 2 * out - prev_ref[...]
    out_ref[...] = out


def apply_field(pos, live, coef, own, near, far, ham, prev=None):
    rows, cols = own.shape
    block_rows, slots, size, _ = ham.shape
    whole = pl.BlockSpec(memory_space=pltpu.VMEM)
    smem = pl.BlockSpec(memory_space=pltpu.SMEM)
    one = pl.BlockSpec((size, cols), lambda i: (i, 0))
    specs = [smem, smem, smem, whole, whole, whole, pl.BlockSpec((1, slots, size, size), lambda i: (i, 0, 0, 0))]
    args = [pos, live, coef, own, near, far, ham]
    if prev is not None:
        specs.append(one)
        args.append(prev)
    return pl.pallas_call(
        functools.partial(field_kernel, prev is not None),
        grid=(block_rows,),
        out_shape=jax.ShapeDtypeStruct((rows, cols), jnp.float32),
        in_specs=specs,
        out_specs=one,
        scratch_shapes=[pltpu.VMEM((3 * rows, cols), jnp.bfloat16)] * 2,
        compiler_params=pltpu.CompilerParams(vmem_limit_bytes=40 * 1024 * 1024),
    )(*args)


def halo(x, count):
    rows = x.shape[0] // PIECES
    swap = [(r, r ^ 1) for r in range(count)]
    pass_on = [(r, (r + 2) % count if r % 2 == 0 else (r - 2) % count) for r in range(count)]
    near = [lax.ppermute(x[p * rows:(p + 1) * rows], "row", swap) for p in range(PIECES)]
    far = [lax.ppermute(p, "row", pass_on) for p in near]
    return jnp.concatenate(near), jnp.concatenate(far)


def on_device(vectors, hamiltonian, column_blocks, live_counts, lower_bound, upper_bound):
    rows_dev, panel_cols = vectors.shape
    block_rows = hamiltonian.shape[0]
    row_count = lax.axis_size("row")
    vec_count = lax.axis_size("vec")
    me = lax.axis_index("row")
    all_cols = panel_cols * vec_count

    rel = (column_blocks - me * block_rows + block_rows) % (block_rows * row_count)
    side = rel // block_rows
    part = jnp.where(side == 1, 0, jnp.where((side == 2) == (me % 2 == 0), 1, 2))
    pos = part * block_rows + rel % block_rows
    centre = (upper_bound[0] + lower_bound[0]) / 2
    radius = (upper_bound[0] - lower_bound[0]) / 2
    coef = jnp.stack([centre, radius])

    near, far = halo(vectors, row_count)
    first = apply_field(pos, live_counts, coef, vectors, near, far, hamiltonian)
    near, far = halo(first, row_count)
    second = apply_field(pos, live_counts, coef, first, near, far, hamiltonian, vectors)

    high = lax.Precision.HIGH
    full_rows = lax.all_gather(second, "vec", axis=1, tiled=True)
    panel = lax.dot_general(full_rows, second, (((0,), (0,)), ((), ())), precision=high, preferred_element_type=jnp.float32)
    panel = lax.psum(panel, "row")
    gram = lax.all_gather(panel, "vec", axis=1, tiled=True)
    energy = jnp.trace(gram)
    scale2 = all_cols / (4 * (energy + 1e-06))
    gram = gram * scale2
    column = jnp.arange(panel_cols)[None, :] + lax.axis_index("vec") * panel_cols
    eye = (jnp.arange(all_cols)[:, None] == column).astype(jnp.float32)

    def times_gram(level, x):
        if level == 0:
            return jnp.dot(gram, x, precision=high)
        return times_gram(level - 1, times_step(level - 1, times_step(level - 1, x)))

    def times_step(level, x):
        return 1.5 * x - 0.5 * times_gram(level, x)

    poly = 1.5 * eye - 0.5 * panel * scale2
    for level in range(1, NS_ITERS):
        poly = times_step(level, poly)
    poly = poly * (jnp.sqrt(scale2) * math.sqrt(rows_dev * row_count))
    return jnp.dot(full_rows, poly, precision=high)


def solution(mesh):
    placed = (P("row", "vec"), P("row", None, None, None), P("row", None), P("row"), P(), P())
    return jax.shard_map(
        on_device, mesh=mesh, in_specs=placed, out_specs=P("row", "vec"), check_vma=False
    )
```

time: 829 us -> 391 us (0.47)
  waiting for transfers between devices: 585 us -> 286 us
  matrix products: 123 us -> 41.9 us
  blocking collectives: 39.6 us -> 0 us
  Pallas kernels: 0 us -> 31.3 us
  local copies, waits for them, and re-layouts: 30.4 us -> 1.83 us
  other arithmetic: 19.2 us -> 4.78 us
    psum x3 -> x1, waiting for transfers between devices: 232 us -> 77.2 us  [on_device(): panel = lax.psum(panel, 'row')]
    dot_general x8 -> x14, matrix products: 123 us -> 41.9 us  [the longest x12 25.3 us: times_gram(): return jnp.dot(gram, x, precision=high)]
    all_gather x3 -> x2, waiting for transfers between devices: 176 us -> 100 us  [the longest x1 63.7 us: on_device(): full_rows = lax.all_gather(second, 'vec', axis=1, tiled=True)]
    ppermute x4 -> x16, waiting for transfers between devices: 178 us -> 108 us  [the longest x8 83.4 us: halo(): lax.ppermute(x[p * rows:(p + 1) * rows], 'row', swap)]
    psum x1 -> x0, blocking collectives: 39.6 us -> none  [on_device(): energy = lax.psum(jnp.sum(second * second), ('row', 'vec'))]
    pallas_call x0 -> x2, Pallas kernels: none -> 31.3 us  [apply_field(): pl.pallas_call(functools.partial(field_kernel, prev is not None), grid=(b...]
    gather x2 -> x0, local copies, waits for them, and re-layouts: 30.3 us -> none  [apply_field(): picked = jnp.take(widened_blocks, local_cols, axis=0)]
  transfers between devices with their start and end apart: 10 -> 19, of which waited for: 10 -> 13; matrix products, arithmetic and copies ran while one was open for 0% -> 0% of each run, Pallas kernels for 0% -> 0%
where the time goes in v1:
time: 391 us; the launch traced here: 388 us
  waiting for transfers between devices  286 us (73%)
  matrix products  41.9 us (11%)
  Pallas kernels  31.3 us (8%)
  between operations  15.4 us (4%)
  starting transfers between devices  7.35 us (2%)
  other arithmetic  4.78 us (1%)
    ppermute x8, waiting for transfers between devices, halo(): lax.ppermute(x[p * rows:(p + 1) * rows], 'row', swap)  83.4 us
    psum x1, waiting for transfers between devices, on_device(): panel = lax.psum(panel, 'row')  77.2 us
    all_gather x1, waiting for transfers between devices, on_device(): full_rows = lax.all_gather(second, 'vec', axis=1, tiled=True)  63.7 us
    all_gather x1, waiting for transfers between devices, on_device(): gram = lax.all_gather(panel, 'vec', axis=1, tiled=True)  36.6 us
    pallas_call x2, Pallas kernels, apply_field(): pl.pallas_call(functools.partial(field_kernel, prev is not None), grid=(b...  31.3 us
    dot_general x12, matrix products, times_gram(): return jnp.dot(gram, x, precision=high)  25.3 us
    ppermute x8, waiting for transfers between devices, halo(): far = [lax.ppermute(p, 'row', pass_on) for p in near]  24.8 us
    dot_general x1, matrix products, on_device(): lax.dot_general(full_rows, second, (((0,), (0,)), ((), ())), precision=hi...  11.7 us
  transfers between devices with their start and end apart: 19, of which 13 were waited for; matrix products, arithmetic and copies ran while one was open for 0% of the time, Pallas kernels for 0%

profile of v1, /device:TPU:23, one launch (start us, length us, event | category | flops | bytes accessed | tf_op | source)
XLA Modules:
  0.0 388.3 jit_solution(8021400994085966119)
XLA Ops:
  6.5 1.7 fusion.47
  8.2 0.3 collective-permute-start
  8.5 1.2 collective-permute-start.1
  9.7 0.3 collective-permute-start.2
  10.0 1.2 collective-permute-start.3
  12.5 8.6 %collective-permute-done = f32[512,256]{1,0:T(8,128)S(1)} collective-permute-done((f32[512,256]{1,0:T(8,128)S(1)}, f32[512,256]{1,0:T(8,128)S(1)}, u32[]{:S(2)}, u32[]{:S(2)}) %collective-permute-start) | collective-permute-done | bytes 524320 | tf_op jit(solution)/shard_map/ppermute | solution.py:87
  21.1 0.2 collective-permute-start.4
  21.2 11.1 %collective-permute-done.1 = f32[512,256]{1,0:T(8,128)S(1)} collective-permute-done((f32[512,256]{1,0:T(8,128)S(1)}, f32[512,256]{1,0:T(8,128)S(1)}, u32[]{:S(2)}, u32[]{:S(2)}) %collective-permute-start.1) | collective-permute-done | bytes 524320 | tf_op jit(solution)/shard_map/ppermute | solution.py:87
  32.3 0.2 collective-permute-start.5
  32.5 11.1 %collective-permute-done.2 = f32[512,256]{1,0:T(8,128)S(1)} collective-permute-done((f32[512,256]{1,0:T(8,128)S(1)}, f32[512,256]{1,0:T(8,128)S(1)}, u32[]{:S(2)}, u32[]{:S(2)}) %collective-permute-start.2) | collective-permute-done | bytes 524320 | tf_op jit(solution)/shard_map/ppermute | solution.py:87
  43.5 0.2 collective-permute-start.6
  43.7 11.2 %collective-permute-done.3 = f32[512,256]{1,0:T(8,128)S(1)} collective-permute-done((f32[512,256]{1,0:T(8,128)S(1)}, f32[512,256]{1,0:T(8,128)S(1)}, u32[]{:S(2)}, u32[]{:S(2)}) %collective-permute-start.3) | collective-permute-done | bytes 524320 | tf_op jit(solution)/shard_map/ppermute | solution.py:87
  54.9 0.2 collective-permute-start.7
  55.2 0.1 pad_maximum_fusion.near_ref
  55.4 11.6 %collective-permute-done.7 = f32[512,256]{1,0:T(8,128)} collective-permute-done((f32[512,256]{1,0:T(8,128)S(1)}, f32[512,256]{1,0:T(8,128)}, u32[]{:S(2)}, u32[]{:S(2)}) %collective-permute-start.7) | collective-permute-done | bytes 524320 | tf_op jit(solution)/shard_map/ppermute | solution.py:88
  67.0 1.3 pad_maximum_fusion.1.far_ref
  68.3 15.1 %shard_map.64.own_ref = f32[2048,256]{1,0:T(8,128)S(1)} custom-call(s32[16,12]{1,0:T(8,128)S(1)} %fusion.42.pos_ref, s32[16]{0:T(128)S(1)} %copy-done.1, f32[2]{0:T(128)S(1)} %pad_maximum_fusion.4.coef_ref, f32[2048,256]{1,0:T(8,128)S(1)} %copy-done, f32[2048,256]{1,0:T(8,128)S(1)} %pad_maximum_fusion.near_ref, f32[2048,256]{1,0:T(8,128)S(1)} %pad_maximum_fusion.1.far_ref, ...), custom_call_target="tpu_custom_call" | custom-call | tf_op jit(solution)/shard_map/pallas_call | solution.py:72
  83.4 0.1 fusion.46
  83.5 0.3 collective-permute-start.8
  83.8 1.3 collective-permute-start.9
  85.1 0.2 collective-permute-start.10
  85.3 1.3 collective-permute-start.11
  86.5 8.2 %collective-permute-done.8 = f32[512,256]{1,0:T(8,128)S(1)} collective-permute-done((f32[512,256]{1,0:T(8,128)S(1)}, f32[512,256]{1,0:T(8,128)S(1)}, u32[]{:S(2)}, u32[]{:S(2)}) %collective-permute-start.8) | collective-permute-done | bytes 524320 | tf_op jit(solution)/shard_map/ppermute | solution.py:87
  94.8 11.1 %collective-permute-done.9 = f32[512,256]{1,0:T(8,128)S(1)} collective-permute-done((f32[512,256]{1,0:T(8,128)S(1)}, f32[512,256]{1,0:T(8,128)S(1)}, u32[]{:S(2)}, u32[]{:S(2)}) %collective-permute-start.9) | collective-permute-done | bytes 524320 | tf_op jit(solution)/shard_map/ppermute | solution.py:87
  106.0 11.1 %collective-permute-done.10 = f32[512,256]{1,0:T(8,128)S(1)} collective-permute-done((f32[512,256]{1,0:T(8,128)S(1)}, f32[512,256]{1,0:T(8,128)S(1)}, u32[]{:S(2)}, u32[]{:S(2)}) %collective-permute-start.10) | collective-permute-done | bytes 524320 | tf_op jit(solution)/shard_map/ppermute | solution.py:87
  117.3 11.1 %collective-permute-done.11 = f32[512,256]{1,0:T(8,128)S(1)} collective-permute-done((f32[512,256]{1,0:T(8,128)S(1)}, f32[512,256]{1,0:T(8,128)S(1)}, u32[]{:S(2)}, u32[]{:S(2)}) %collective-permute-start.11) | collective-permute-done | bytes 524320 | tf_op jit(solution)/shard_map/ppermute | solution.py:87
  128.5 0.1 pad_maximum_fusion.2.near_ref
  128.7 13.2 %collective-permute-done.15 = f32[512,256]{1,0:T(8,128)S(1)} collective-permute-done((f32[512,256]{1,0:T(8,128)S(1)}, f32[512,256]{1,0:T(8,128)S(1)}, u32[]{:S(2)}, u32[]{:S(2)}) %collective-permute-start.15) | collective-permute-done | bytes 524320 | tf_op jit(solution)/shard_map/ppermute | solution.py:88
  142.0 16.2 %shard_map.65 = f32[2048,256]{1,0:T(8,128)} custom-call(s32[16,12]{1,0:T(8,128)S(1)} %fusion.42.pos_ref, s32[16]{0:T(128)S(1)} %copy-done.1, f32[2]{0:T(128)S(1)} %pad_maximum_fusion.4.coef_ref, f32[2048,256]{1,0:T(8,128)S(1)} %shard_map.64.own_ref, f32[2048,256]{1,0:T(8,128)S(1)} %pad_maximum_fusion.2.near_ref, f32[2048,256]{1,0:T(8,128)S(1)} %pad_maximum_fusion.3.far_ref, ...), custom_call_target="tpu_custom_call" | custom-call | tf_op jit(solution)/shard_map/pallas_call | solution.py:72
  158.2 63.7 %all-gather.3.cloned.1.call-done = f32[2048,1024]{1,0:T(8,128)} async-done(((f32[2048,256]{1,0:T(8,128)}), f32[2048,1024]{1,0:T(8,128)}) %all-gather.3.cloned.1.call-update) | async-done | bytes 8388624 | tf_op jit(solution)/shard_map/all_gather | solution.py:114
  221.9 11.7 %fusion.48 = f32[1024,256]{1,0:T(8,128)} fusion(f32[2048,1024]{1,0:T(8,128)} %all-gather.3.cloned.1.call-done, f32[2048,256]{1,0:T(8,128)} %shard_map.65), kind=kOutput, calls=%fused_computation.68 | convolution fusion | flops 3221225472 | bytes 11534336 | tf_op jit(solution)/shard_map/dot_general | solution.py:115
  233.7 0.2 all-gather.5.cloned.1.call-start
  233.9 77.2 %all-reduce.2.cloned.1.call-done = f32[1024,256]{1,0:T(8,128)} async-done(((f32[1024,256]{1,0:T(8,128)}), f32[1024,256]{1,0:T(8,128)}) %all-reduce.2.cloned.1.call-update) | async-done | bytes 1048592 | tf_op jit(solution)/shard_map/psum | solution.py:116
  311.1 36.6 %all-gather.5.cloned.1.call-done = f32[1024,1024]{1,0:T(8,128)} async-done(((f32[1024,256]{1,0:T(8,128)}), f32[1024,1024]{1,0:T(8,128)}) %all-gather.5.cloned.1.call-update) | async-done | bytes 4194320 | tf_op jit(solution)/shard_map/all_gather | solution.py:117
  347.7 2.9 select_reduce_fusion
  351.4 4.4 %fusion.13 = f32[1024,256]{1,0:T(8,128)S(1)} fusion(f32[1024,1024]{1,0:T(8,128)} %all-gather.5.cloned.1.call-done, f32[]{:T(128)S(6)} %div.27, f32[1024,256]{1,0:T(8,128)S(1)} %copy-done.3, f32[]{:T(128)S(6)} %mul.104, s32[256]{0:T(256)S(1)} %iota_add_fusion), kind=kOutput, calls=%fused_computation.20 | convolution fusion | flops 1614544896 | bytes 6292488 | tf_op jit(solution)/shard_map/dot_general | solution.py:126
  355.8 1.9 fusion.15
  357.7 1.9 fusion.17
  359.6 1.9 fusion.19
  361.5 1.9 fusion.21
  363.4 1.9 fusion.23
  365.3 2.1 fusion.25
  367.4 1.9 fusion.27
  369.3 1.9 fusion.29
  371.2 1.9 fusion.31
  373.1 1.9 fusion.33
  375.0 1.9 fusion.36
  376.9 4.9 %fusion.49 = f32[2048,256]{1,0:T(8,128)} fusion(f32[2048,1024]{1,0:T(8,128)S(1)} %bitcast.16, f32[1024,256]{1,0:T(8,128)S(1)} %fusion.36), kind=kOutput, calls=%fused_computation.69 | convolution fusion | flops 3221225472 | bytes 11534336 | tf_op jit(solution)/shard_map/dot_general | solution.py:136
  (34 shorter events, 0.8 us)
Async XLA Ops:
  6.5 48.6 %copy-start.4 = (s32[16,12]{1,0:T(8,128)S(1)}, s32[16,12]{1,0:T(8,128)}, u32[]{:S(2)}) copy-start(s32[16,12]{1,0:T(8,128)} %param.8) | copy-start | bytes 2308
  6.5 215.4 %all-gather.3.cloned.1.call-start = ((), (), s32[]{:S(2)}) async-start(), calls=%async_computation | async-start | bytes 10485760 | tf_op jit(solution)/shard_map/all_gather | solution.py:114
  8.2 12.9 %collective-permute-start = (f32[512,256]{1,0:T(8,128)S(1)}, f32[512,256]{1,0:T(8,128)S(1)}, u32[]{:S(2)}, u32[]{:S(2)}) collective-permute-start(f32[512,256]{1,0:T(8,128)S(1)} %get-tuple-element.9), channel_id=1, source_target_pairs={{0,4},{4,0},{8,12},{12,8},{16,20},{20,16},{24,28},{28,24},{1,5},{5... | collective-permute-start | bytes 1572872 | tf_op jit(solution)/shard_map/ppermute | solution.py:87
  8.5 23.8 %collective-permute-start.1 = (f32[512,256]{1,0:T(8,128)S(1)}, f32[512,256]{1,0:T(8,128)S(1)}, u32[]{:S(2)}, u32[]{:S(2)}) collective-permute-start(f32[512,256]{1,0:T(8,128)S(1)} %get-tuple-element.12), channel_id=1, source_target_pairs={{0,4},{4,0},{8,12},{12,8},{16,20},{20,16},{24,28},{28,24},{1,5},{5... | collective-permute-start | bytes 1572872 | tf_op jit(solution)/shard_map/ppermute | solution.py:87
  9.7 33.8 %collective-permute-start.2 = (f32[512,256]{1,0:T(8,128)S(1)}, f32[512,256]{1,0:T(8,128)S(1)}, u32[]{:S(2)}, u32[]{:S(2)}) collective-permute-start(f32[512,256]{1,0:T(8,128)S(1)} %get-tuple-element.11), channel_id=1, source_target_pairs={{0,4},{4,0},{8,12},{12,8},{16,20},{20,16},{24,28},{28,24},{1,5},{5... | collective-permute-start | bytes 1572872 | tf_op jit(solution)/shard_map/ppermute | solution.py:87
  10.0 44.9 %collective-permute-start.3 = (f32[512,256]{1,0:T(8,128)S(1)}, f32[512,256]{1,0:T(8,128)S(1)}, u32[]{:S(2)}, u32[]{:S(2)}) collective-permute-start(f32[512,256]{1,0:T(8,128)S(1)} %get-tuple-element.10), channel_id=1, source_target_pairs={{0,4},{4,0},{8,12},{12,8},{16,20},{20,16},{24,28},{28,24},{1,5},{5... | collective-permute-start | bytes 1572872 | tf_op jit(solution)/shard_map/ppermute | solution.py:87
  21.1 34.3 %collective-permute-start.4 = (f32[512,256]{1,0:T(8,128)S(1)}, f32[512,256]{1,0:T(8,128)S(1)}, u32[]{:S(2)}, u32[]{:S(2)}) collective-permute-start(f32[512,256]{1,0:T(8,128)S(1)} %collective-permute-done), channel_id=1, source_target_pairs={{0,8},{4,28},{8,16},{12,4},{16,24},{20,12},{24,0},{28,20},{1,9},{5... | collective-permute-start | bytes 1572872 | tf_op jit(solution)/shard_map/ppermute | solution.py:88
  32.3 23.0 %collective-permute-start.5 = (f32[512,256]{1,0:T(8,128)S(1)}, f32[512,256]{1,0:T(8,128)S(1)}, u32[]{:S(2)}, u32[]{:S(2)}) collective-permute-start(f32[512,256]{1,0:T(8,128)S(1)} %collective-permute-done.1), channel_id=1, source_target_pairs={{0,8},{4,28},{8,16},{12,4},{16,24},{20,12},{24,0},{28,20},{1,9},{5... | collective-permute-start | bytes 1572872 | tf_op jit(solution)/shard_map/ppermute | solution.py:88
  43.5 11.8 %collective-permute-start.6 = (f32[512,256]{1,0:T(8,128)S(1)}, f32[512,256]{1,0:T(8,128)}, u32[]{:S(2)}, u32[]{:S(2)}) collective-permute-start(f32[512,256]{1,0:T(8,128)S(1)} %collective-permute-done.2), channel_id=1, source_target_pairs={{0,8},{4,28},{8,16},{12,4},{16,24},{20,12},{24,0},{28,20},{1,9},{5... | collective-permute-start | bytes 1572872 | tf_op jit(solution)/shard_map/ppermute | solution.py:88
  54.9 12.1 %collective-permute-start.7 = (f32[512,256]{1,0:T(8,128)S(1)}, f32[512,256]{1,0:T(8,128)}, u32[]{:S(2)}, u32[]{:S(2)}) collective-permute-start(f32[512,256]{1,0:T(8,128)S(1)} %collective-permute-done.3), channel_id=1, source_target_pairs={{0,8},{4,28},{8,16},{12,4},{16,24},{20,12},{24,0},{28,20},{1,9},{5... | collective-permute-start | bytes 1572872 | tf_op jit(solution)/shard_map/ppermute | solution.py:88
  55.1 13.1 %copy-start = (f32[2048,256]{1,0:T(8,128)S(1)}, f32[2048,256]{1,0:T(8,128)}, u32[]{:S(2)}) copy-start(f32[2048,256]{1,0:T(8,128)} %rest_0_.1) | copy-start | bytes 6291460
  55.2 13.1 %copy-start.1 = (s32[16]{0:T(128)S(1)}, s32[16]{0:T(128)}, u32[]{:S(2)}) copy-start(s32[16]{0:T(128)} %live_ref.3) | copy-start | bytes 196
  83.5 11.2 %collective-permute-start.8 = (f32[512,256]{1,0:T(8,128)S(1)}, f32[512,256]{1,0:T(8,128)S(1)}, u32[]{:S(2)}, u32[]{:S(2)}) collective-permute-start(f32[512,256]{1,0:T(8,128)S(1)} %get-tuple-element.5), channel_id=1, source_target_pairs={{0,4},{4,0},{8,12},{12,8},{16,20},{20,16},{24,28},{28,24},{1,5},{5... | collective-permute-start | bytes 1572872 | tf_op jit(solution)/shard_map/ppermute | solution.py:87
  83.8 22.1 %collective-permute-start.9 = (f32[512,256]{1,0:T(8,128)S(1)}, f32[512,256]{1,0:T(8,128)S(1)}, u32[]{:S(2)}, u32[]{:S(2)}) collective-permute-start(f32[512,256]{1,0:T(8,128)S(1)} %get-tuple-element.8), channel_id=1, source_target_pairs={{0,4},{4,0},{8,12},{12,8},{16,20},{20,16},{24,28},{28,24},{1,5},{5... | collective-permute-start | bytes 1572872 | tf_op jit(solution)/shard_map/ppermute | solution.py:87
  85.1 32.1 %collective-permute-start.10 = (f32[512,256]{1,0:T(8,128)S(1)}, f32[512,256]{1,0:T(8,128)S(1)}, u32[]{:S(2)}, u32[]{:S(2)}) collective-permute-start(f32[512,256]{1,0:T(8,128)S(1)} %get-tuple-element.7), channel_id=1, source_target_pairs={{0,4},{4,0},{8,12},{12,8},{16,20},{20,16},{24,28},{28,24},{1,5},{5... | collective-permute-start | bytes 1572872 | tf_op jit(solution)/shard_map/ppermute | solution.py:87
  85.3 43.1 %collective-permute-start.11 = (f32[512,256]{1,0:T(8,128)S(1)}, f32[512,256]{1,0:T(8,128)S(1)}, u32[]{:S(2)}, u32[]{:S(2)}) collective-permute-start(f32[512,256]{1,0:T(8,128)S(1)} %get-tuple-element.6), channel_id=1, source_target_pairs={{0,4},{4,0},{8,12},{12,8},{16,20},{20,16},{24,28},{28,24},{1,5},{5... | collective-permute-start | bytes 1572872 | tf_op jit(solution)/shard_map/ppermute | solution.py:87
  94.7 34.0 %collective-permute-start.12 = (f32[512,256]{1,0:T(8,128)S(1)}, f32[512,256]{1,0:T(8,128)S(1)}, u32[]{:S(2)}, u32[]{:S(2)}) collective-permute-start(f32[512,256]{1,0:T(8,128)S(1)} %collective-permute-done.8), channel_id=1, source_target_pairs={{0,8},{4,28},{8,16},{12,4},{16,24},{20,12},{24,0},{28,20},{1,9},{5... | collective-permute-start | bytes 1572872 | tf_op jit(solution)/shard_map/ppermute | solution.py:88
  105.9 22.7 %collective-permute-start.13 = (f32[512,256]{1,0:T(8,128)S(1)}, f32[512,256]{1,0:T(8,128)S(1)}, u32[]{:S(2)}, u32[]{:S(2)}) collective-permute-start(f32[512,256]{1,0:T(8,128)S(1)} %collective-permute-done.9), channel_id=1, source_target_pairs={{0,8},{4,28},{8,16},{12,4},{16,24},{20,12},{24,0},{28,20},{1,9},{5... | collective-permute-start | bytes 1572872 | tf_op jit(solution)/shard_map/ppermute | solution.py:88
  117.2 11.5 %collective-permute-start.14 = (f32[512,256]{1,0:T(8,128)S(1)}, f32[512,256]{1,0:T(8,128)S(1)}, u32[]{:S(2)}, u32[]{:S(2)}) collective-permute-start(f32[512,256]{1,0:T(8,128)S(1)} %collective-permute-done.10), channel_id=1, source_target_pairs={{0,8},{4,28},{8,16},{12,4},{16,24},{20,12},{24,0},{28,20},{1,9},{5... | collective-permute-start | bytes 1572872 | tf_op jit(solution)/shard_map/ppermute | solution.py:88
  128.4 13.4 %collective-permute-start.15 = (f32[512,256]{1,0:T(8,128)S(1)}, f32[512,256]{1,0:T(8,128)S(1)}, u32[]{:S(2)}, u32[]{:S(2)}) collective-permute-start(f32[512,256]{1,0:T(8,128)S(1)} %collective-permute-done.11), channel_id=1, source_target_pairs={{0,8},{4,28},{8,16},{12,4},{16,24},{20,12},{24,0},{28,20},{1,9},{5... | collective-permute-start | bytes 1572872 | tf_op jit(solution)/shard_map/ppermute | solution.py:88
  158.2 152.9 %all-reduce.2.cloned.1.call-start = ((), (), s32[]{:S(2)}) async-start(), calls=%async_computation.1 | async-start | bytes 2097152 | tf_op jit(solution)/shard_map/psum | solution.py:116
  233.7 114.0 %all-gather.5.cloned.1.call-start = ((), (), s32[]{:S(2)}) async-start(), calls=%async_computation.2 | async-start | bytes 5242880 | tf_op jit(solution)/shard_map/all_gather | solution.py:117
  311.1 40.3 %copy-start.3 = (f32[1024,256]{1,0:T(8,128)S(1)}, f32[1024,256]{1,0:T(8,128)}, u32[]{:S(2)}) copy-start(f32[1024,256]{1,0:T(8,128)} %all-reduce.2.cloned.1.call-done) | copy-start | bytes 3145732
  351.4 4.4 %copy-start.2 = (f32[1024,1024]{1,0:T(8,128)S(1)}, f32[1024,1024]{1,0:T(8,128)}, u32[]{:S(2)}) copy-start(f32[1024,1024]{1,0:T(8,128)} %all-gather.5.cloned.1.call-done) | copy-start | bytes 12582916
  371.2 5.7 %slice-start = ((s8[8388608]{0:T(1024)(128)(4,1)}), s8[4194304]{0:T(1024)(128)(4,1)S(1)}, s32[]{:S(2)}) async-start(s8[8388608]{0:T(1024)(128)(4,1)} %bitcast.15), calls=%async_computation.3 | async-start | bytes 8388608
  373.1 3.8 slice-start.1
Sparse Core Ops, SparseCore 0:
  158.3 63.5 all-gather.2
  233.8 77.2 all-reduce.1
  312.7 34.9 all-gather.4

commit v2 on v1

v2 whole, which is shorter than its diff:
```python
import functools
import math

import jax
import jax.numpy as jnp
from jax import lax
from jax.experimental import pallas as pl
from jax.experimental.pallas import tpu as pltpu
from jax.sharding import PartitionSpec as P

NS_ITERS = 3
PIECES = 4
MESH = pl.DeviceIdType.MESH


def split(x):
    hi = x.astype(jnp.bfloat16)
    return hi, (x - hi.astype(jnp.float32)).astype(jnp.bfloat16)


def dot(a, b):
    return jnp.dot(a, b, preferred_element_type=jnp.float32)


def filter_kernel(row_count, vec_count, width, pos_ref, live_ref, coef_ref, vec_ref, ham_ref, full_ref,
                  ham, mats, near, far, first, hi_ref, lo_ref, ham_sem,
                  swap_send, swap_recv, pass_send, pass_recv, side_send, side_recv, over_send, over_recv,
                  relay_send, relay_recv):
    row, vec = lax.axis_index("row"), lax.axis_index("vec")
    rows, cols = vec_ref.shape
    block_rows, slots, size, _ = ham.shape
    chunks = cols // width
    piece = rows // PIECES
    even = 1 - row % 2
    partner = row + 2 * even - 1
    onward = (row + 4 * even - 2 + row_count) % row_count
    backward = (row - 4 * even + 2 + row_count) % row_count
    sibling = vec + 1 - 2 * (vec % 2)
    overs = [(vec + 2 * d) % vec_count for d in range(1, vec_count // 2)]
    sources = [(vec - 2 * d + vec_count) % vec_count for d in range(1, vec_count // 2)]

    copy = pltpu.make_async_copy(ham_ref, ham, ham_sem)
    copy.start()
    barrier = pltpu.get_barrier_semaphore()
    peers = [(partner, vec), (onward, vec), (backward, vec), (row, sibling)] + [(row, v) for v in overs]
    for peer in peers:
        pl.semaphore_signal(barrier, inc=1, device_id=peer, device_id_type=MESH)
    pl.semaphore_wait(barrier, len(peers))

    def part(q):
        return pl.ds(q * piece, piece)

    def columns(c, v):
        return pl.ds(pl.multiple_of((c * vec_count + v) * width, width), width)

    def own_at(stage, c, q):
        return first.at[c, part(q)] if stage else vec_ref.at[part(q), pl.ds(c * width, width)]

    def swap(stage, c, q):
        return pltpu.make_async_remote_copy(
            own_at(stage, c, q), near.at[stage, c, part(q)], swap_send.at[stage, c, q], swap_recv.at[stage, c, q],
            device_id=(partner, vec), device_id_type=MESH)

    def pass_on(stage, c, q):
        return pltpu.make_async_remote_copy(
            near.at[stage, c, part(q)], far.at[stage, c, part(q)], pass_send.at[stage, c, q],
            pass_recv.at[stage, c, q], device_id=(onward, vec), device_id_type=MESH)

    def across(c, q, v, send, recv, to):
        at = full_ref.at[part(q), columns(c, v)]
        return pltpu.make_async_remote_copy(at, at, send, recv, device_id=(row, to), device_id_type=MESH)

    def side(c, q):
        return across(c, q, vec, side_send.at[c, q], side_recv.at[c, q], sibling)

    def over(c, q, d):
        return across(c, q, vec, over_send.at[c, q, d], over_recv.at[c, q, d], overs[d])

    def relay(c, q, d):
        return across(c, q, sources[d], relay_send.at[c, q, d], relay_recv.at[c, q, d], sibling)

    every = [(c, q) for c in range(chunks) for q in range(PIECES)]
    for c, q in every:
        swap(0, c, q).start()

    copy.wait()

    @pl.loop(0, block_rows)
    def _(i):
        for k in range(0, slots, 2):
            pair = [ham[i, s] * live_ref[i, s] for s in (k, k + 1)]
            hi, lo = split(jnp.concatenate(pair, axis=1))
            mats[i, k // 2, pl.ds(0, size), :] = hi
            mats[i, k // 2, pl.ds(size, size), :] = lo

    def spread(read, place, q):
        @pl.loop(0, piece // size)
        def _(b):
            at = pl.multiple_of(q * piece + b * size, size)
            hi, lo = split(read(pl.ds(at, size)))
            to = (place * rows + q * piece) // size + b
            hi_ref[to] = hi
            lo_ref[to] = lo

    for stage in range(2):
        for c in range(chunks):
            wide = pl.ds(c * width, width)

            def own(at):
                return first[c, at, :] if stage else vec_ref[at, wide]

            for q in range(PIECES):
                spread(own, 0, q)
            for q in range(PIECES):
                swap(stage, c, q).wait_recv()
                pass_on(stage, c, q).start()
                spread(lambda at: near[stage, c, at, :], 1, q)
            for q in range(PIECES):
                pass_on(stage, c, q).wait_recv()
                spread(lambda at: far[stage, c, at, :], 2, q)

            @pl.loop(0, block_rows)
            def _(i):
                total = jnp.zeros((size, width), jnp.float32)
                for k in range(0, slots, 2):
                    vhi = jnp.concatenate([hi_ref[pos_ref[i, s]] for s in (k, k + 1)], axis=0)
                    vlo = jnp.concatenate([lo_ref[pos_ref[i, s]] for s in (k, k + 1)], axis=0)
                    both = dot(mats[i, k // 2], vhi)
                    total += both[:size] + both[size:] + dot(mats[i, k // 2, pl.ds(0, size), :], vlo)
                at = pl.ds(pl.multiple_of(i * size, size), size)
                out = (total - coef_ref[0] * own(at)) / coef_ref[1]
                if stage:
                    full_ref[at, columns(c, vec)] = 2 * out - vec_ref[at, wide]
                else:
                    first[c, at, :] = out

            for q in range(PIECES):
                if stage:
                    for d in range(len(overs)):
                        over(c, q, d).start()
                    side(c, q).start()
                else:
                    swap(1, c, q).start()

    for c, q in every:
        for d in range(len(overs)):
            over(c, q, d).wait_recv()
            relay(c, q, d).start()
    for c, q in every:
        side(c, q).wait()
        for d in range(len(overs)):
            over(c, q, d).wait_send()
            relay(c, q, d).wait()
        for stage in range(2):
            swap(stage, c, q).wait_send()
            pass_on(stage, c, q).wait_send()


def filtered_rows(row_count, vec_count, width, pos, live, coef, vectors, ham):
    rows, cols = vectors.shape
    block_rows, slots, size, _ = ham.shape
    chunks = cols // width
    smem = pl.BlockSpec(memory_space=pltpu.SMEM)
    vmem = pl.BlockSpec(memory_space=pltpu.VMEM)
    dma = pltpu.SemaphoreType.DMA
    others = max(1, vec_count // 2 - 1)
    return pl.pallas_call(
        functools.partial(filter_kernel, row_count, vec_count, width),
        out_shape=jax.ShapeDtypeStruct((rows, cols * vec_count), jnp.float32),
        in_specs=[smem, smem, smem, vmem, pl.BlockSpec(memory_space=pl.ANY)],
        out_specs=vmem,
        scratch_shapes=[
            pltpu.VMEM(ham.shape, jnp.float32),
            pltpu.VMEM((block_rows, slots // 2, 2 * size, 2 * size), jnp.bfloat16),
            pltpu.VMEM((2, chunks, rows, width), jnp.float32),
            pltpu.VMEM((2, chunks, rows, width), jnp.float32),
            pltpu.VMEM((chunks, rows, width), jnp.float32),
            pltpu.VMEM((3 * block_rows, size, width), jnp.bfloat16),
            pltpu.VMEM((3 * block_rows, size, width), jnp.bfloat16),
            dma,
            dma((2, chunks, PIECES)), dma((2, chunks, PIECES)),
            dma((2, chunks, PIECES)), dma((2, chunks, PIECES)),
            dma((chunks, PIECES)), dma((chunks, PIECES)),
            dma((chunks, PIECES, others)), dma((chunks, PIECES, others)),
            dma((chunks, PIECES, others)), dma((chunks, PIECES, others)),
        ],
        compiler_params=pltpu.CompilerParams(
            collective_id=0, has_side_effects=True, vmem_limit_bytes=58 * 1024 * 1024
        ),
    )(pos, live, coef, vectors, ham)


def on_device(vectors, hamiltonian, column_blocks, live_counts, lower_bound, upper_bound):
    rows_dev, panel_cols = vectors.shape
    block_rows = hamiltonian.shape[0]
    row_count = lax.axis_size("row")
    vec_count = lax.axis_size("vec")
    me = lax.axis_index("row")
    all_cols = panel_cols * vec_count

    rel = (column_blocks - me * block_rows + block_rows) % (block_rows * row_count)
    side = rel // block_rows
    part = jnp.where(side == 1, 0, jnp.where((side == 2) == (me % 2 == 0), 1, 2))
    pos = part * block_rows + rel % block_rows
    slots = column_blocks.shape[1]
    live = (jnp.arange(slots, dtype=jnp.int32)[None, :] < live_counts[:, None]).astype(jnp.float32)
    centre = (upper_bound[0] + lower_bound[0]) / 2
    radius = (upper_bound[0] - lower_bound[0]) / 2
    coef = jnp.stack([centre, radius])

    width = max(128, panel_cols // 2)
    full_rows = filtered_rows(
        row_count, vec_count, width, pos, live, coef, vectors, hamiltonian
    )

    high = lax.Precision.HIGH
    span = width * vec_count
    own = jnp.concatenate([
        lax.dynamic_slice_in_dim(full_rows, c * span + lax.axis_index("vec") * width, width, axis=1)
        for c in range(panel_cols // width)
    ], axis=1)
    panel = lax.dot_general(
        full_rows, own, (((0,), (0,)), ((), ())), precision=high, preferred_element_type=jnp.float32
    )
    panel = lax.psum(panel, "row")
    panels = lax.all_gather(panel, "vec")
    gram = jnp.concatenate(
        [panels[v][:, c:c + width] for c in range(0, panel_cols, width) for v in range(vec_count)], axis=1
    )
    energy = jnp.trace(gram)
    scale2 = all_cols / (4 * (energy + 1e-06))
    gram = gram * scale2
    local = jnp.arange(panel_cols)
    column = local // width * (width * vec_count) + lax.axis_index("vec") * width + local % width
    eye = (jnp.arange(all_cols)[:, None] == column[None, :]).astype(jnp.float32)

    def times_gram(level, x):
        if level == 0:
            return jnp.dot(gram, x, precision=high)
        return times_gram(level - 1, times_step(level - 1, times_step(level - 1, x)))

    def times_step(level, x):
        return 1.5 * x - 0.5 * times_gram(level, x)

    poly = 1.5 * eye - 0.5 * panel * scale2
    for level in range(1, NS_ITERS):
        poly = times_step(level, poly)
    poly = poly * (jnp.sqrt(scale2) * math.sqrt(rows_dev * row_count))
    return jnp.dot(full_rows, poly, precision=high)


def solution(mesh):
    placed = (P("row", "vec"), P("row", None, None, None), P("row", None), P("row"), P(), P())
    return jax.shard_map(
        on_device, mesh=mesh, in_specs=placed, out_specs=P("row", "vec"), check_vma=False
    )
```

time: 391 us -> 350 us (0.90)
  waiting for transfers between devices: 286 us -> 117 us
  Pallas kernels: 31.3 us -> 153 us
  local copies, waits for them, and re-layouts: 1.83 us -> 12.6 us
  starting transfers between devices: 7.35 us -> 0.22 us
    pallas_call x2 -> x1, Pallas kernels: 31.3 us -> 153 us  [filtered_rows(): pl.pallas_call(functools.partial(filter_kernel, row_count, vec_count, wid...]
    ppermute x16 -> x0, waiting for transfers between devices: 108 us -> none  [the longest x8 83.4 us: halo(): lax.ppermute(x[p * rows:(p + 1) * rows], 'row', swap)]
    all_gather x2 -> x1, waiting for transfers between devices: 100 us -> 36.6 us  [on_device(): panels = lax.all_gather(panel, 'vec')]
    unnamed x14 -> x13, local copies, waits for them, and re-layouts: 0.03 us -> 9.77 us
    ppermute x16 -> x0, starting transfers between devices: 7.08 us -> none  [the longest x8 5.99 us: halo(): lax.ppermute(x[p * rows:(p + 1) * rows], 'row', swap)]
  transfers between devices with their start and end apart: 19 -> 2, of which waited for: 13 -> 2; matrix products, arithmetic and copies ran while one was open for 0% -> 0% of each run, Pallas kernels for 0% -> 0%
where the time goes in v2:
time: 350 us; the launch traced here: 347 us
  Pallas kernels  153 us (44%)
  waiting for transfers between devices  117 us (33%)
  matrix products  44.8 us (13%)
  between operations  15.7 us (4%)
  local copies, waits for them, and re-layouts  12.6 us (4%)
  other arithmetic  4.02 us (1%)
    pallas_call x1, Pallas kernels, filtered_rows(): pl.pallas_call(functools.partial(filter_kernel, row_count, vec_count, wid...  153 us
    psum x1, waiting for transfers between devices, on_device(): panel = lax.psum(panel, 'row')  80.5 us
    all_gather x1, waiting for transfers between devices, on_device(): panels = lax.all_gather(panel, 'vec')  36.6 us
    dot_general x12, matrix products, times_gram(): return jnp.dot(gram, x, precision=high)  27.5 us
    dot_general x1, matrix products, on_device(): lax.dot_general(full_rows, own, (((0,), (0,)), ((), ())), precision=high,...  10.2 us
    unnamed x13, local copies, waits for them, and re-layouts  9.77 us
    dot_general x1, matrix products, on_device(): return jnp.dot(full_rows, poly, precision=high)  7.17 us
  transfers between devices with their start and end apart: 2, of which 2 were waited for; matrix products, arithmetic and copies ran while one was open for 0% of the time, Pallas kernels for 0%

profile of v2, /device:TPU:23, one launch (start us, length us, event | category | flops | bytes accessed | tf_op | source)
XLA Modules:
  0.0 347.3 jit_solution(13611166613493438337)
XLA Ops:
  6.5 0.0 all-reduce.2.cloned.1.call-start
  7.8 1.3 fusion.48.live_ref
  9.2 0.6 pad_maximum_fusion.coef_ref
  9.8 1.3 fusion.46.pos_ref
  11.1 152.8 %shard_map.64 = f32[2048,1024]{1,0:T(8,128)} custom-call(s32[16,12]{1,0:T(8,128)} %fusion.46.pos_ref, f32[16,12]{1,0:T(8,128)} %fusion.48.live_ref, f32[2]{0:T(128)} %pad_maximum_fusion.coef_ref, f32[2048,256]{1,0:T(8,128)} %vec_ref.1, f32[16,12,128,128]{3,2,1,0:T(8,128)} %ham_ref.1), custom_call_target="tpu_custom_call" | custom-call | tf_op jit(solution)/shard_map/pallas_call | solution.py:167
  164.0 1.7 constant_dynamic-slice_fusion.1
  165.7 10.2 %fusion = f32[1024,256]{1,0:T(8,128)} fusion(f32[2048,1024]{1,0:T(8,128)} %shard_map.64, f32[2048,128]{1,0:T(8,128)S(1)} %get-tuple-element.6, f32[2048,128]{1,0:T(8,128)S(1)} %get-tuple-element.5), kind=kOutput, calls=%fused_computation.2 | convolution fusion | flops 3221749760 | bytes 11534336 | tf_op jit(solution)/shard_map/dot_general | solution.py:222
  175.9 0.0 all-reduce.2.cloned.1.call-update
  175.9 0.2 all-gather.3.cloned.1.call-start
  176.1 80.5 %all-reduce.2.cloned.1.call-done = f32[1024,256]{1,0:T(8,128)} async-done(((f32[1024,256]{1,0:T(8,128)}), f32[1024,256]{1,0:T(8,128)}) %all-reduce.2.cloned.1.call-update) | async-done | bytes 1048592 | tf_op jit(solution)/shard_map/psum | solution.py:225
  256.7 0.0 all-gather.3.cloned.1.call-update
  256.7 36.6 %all-gather.3.cloned.1.call-done = f32[4096,256]{1,0:T(8,128)} async-done(((f32[1024,256]{1,0:T(8,128)}), f32[4096,256]{1,0:T(8,128)}) %all-gather.3.cloned.1.call-update) | async-done | bytes 4194320 | tf_op jit(solution)/shard_map/all_gather | solution.py:226
  293.3 1.1 slice_dynamic-update-slice_fusion.7
  294.4 1.1 slice_dynamic-update-slice_fusion.6
  295.5 1.1 slice_dynamic-update-slice_fusion.5
  296.6 1.1 slice_dynamic-update-slice_fusion.4
  297.7 0.0 copy-start.2
  297.8 1.2 slice_dynamic-update-slice_fusion.3
  298.9 1.1 slice_dynamic-update-slice_fusion.2
  300.1 1.1 slice_dynamic-update-slice_fusion.1
  301.2 1.1 slice_dynamic-update-slice_fusion
  302.3 0.0 copy-start
  302.3 1.9 copy-done
  304.2 0.7 select_reduce_fusion
  305.7 0.0 copy-done.2
  305.7 0.0 copy-start.1
  305.7 4.4 %fusion.17 = f32[1024,256]{1,0:T(8,128)S(1)} fusion(f32[1024,1024]{1,0:T(8,128)} %copy-done, f32[]{:T(128)S(6)} %div.37, f32[1024,256]{1,0:T(8,128)S(1)} %copy-done.2, f32[]{:T(128)S(6)} %mul.118, s32[256]{0:T(256)S(1)} %fusion.51), kind=kOutput, calls=%fused_computation.20 | convolution fusion | flops 1614544896 | bytes 6292488 | tf_op jit(solution)/shard_map/dot_general | solution.py:239
  310.1 0.0 copy-done.1
  310.1 1.9 fusion.19
  312.0 1.9 fusion.21
  313.9 1.8 fusion.23
  315.8 1.9 fusion.25
  317.7 1.9 fusion.27
  319.5 2.1 fusion.29
  321.7 1.9 fusion.31
  323.6 1.9 fusion.33
  325.4 1.9 fusion.35
  327.3 1.9 fusion.37
  329.2 4.1 %fusion.40 = f32[1024,256]{1,0:T(8,128)S(1)} fusion(f32[1024,256]{1,0:T(8,128)S(1)} %fusion.37, f32[1024,1024]{1,0:T(8,128)} %copy-done, f32[]{:T(128)S(6)} %div.37, f32[1024,256]{1,0:T(8,128)S(1)} %fusion.21, f32[]{:T(128)S(6)} %mul.143), kind=kOutput, calls=%fused_computation.43 | convolution fusion | flops 1612709888 | bytes 7340040 | tf_op jit(solution)/shard_map/dot_general | solution.py:239
  333.3 7.2 %fusion.57 = f32[2048,256]{1,0:T(8,128)} fusion(f32[2048,1024]{1,0:T(8,128)} %shard_map.64, f32[1024,256]{1,0:T(8,128)S(1)} %fusion.40), kind=kOutput, calls=%fused_computation.88 | convolution fusion | flops 3221225472 | bytes 11534336 | tf_op jit(solution)/shard_map/dot_general | solution.py:249
  (1 shorter events, 0.0 us)
Async XLA Ops:
  6.5 250.1 %all-reduce.2.cloned.1.call-start = ((), (), s32[]{:S(2)}) async-start(), calls=%async_computation | async-start | bytes 2097152 | tf_op jit(solution)/shard_map/psum | solution.py:225
  175.9 117.4 %all-gather.3.cloned.1.call-start = ((), (), s32[]{:S(2)}) async-start(), calls=%async_computation.1 | async-start | bytes 5242880 | tf_op jit(solution)/shard_map/all_gather | solution.py:226
  297.7 8.0 %copy-start.2 = (f32[1024,256]{1,0:T(8,128)S(1)}, f32[1024,256]{1,0:T(8,128)}, u32[]{:S(2)}) copy-start(f32[1024,256]{1,0:T(8,128)} %all-reduce.2.cloned.1.call-done) | copy-start | bytes 3145732
  302.3 1.9 copy-start
  305.7 4.4 %copy-start.1 = (f32[1024,1024]{1,0:T(8,128)S(1)}, f32[1024,1024]{1,0:T(8,128)}, u32[]{:S(2)}) copy-start(f32[1024,1024]{1,0:T(8,128)} %copy-done) | copy-start | bytes 12582916
Sparse Core Ops, SparseCore 0:
  176.0 80.5 all-reduce.1
  258.3 34.9 all-gather.2

commit v3 on v2

--- a/solution.py
+++ b/solution.py
@@ -190,6 +190,152 @@
     )(pos, live, coef, vectors, ham)
 
 
+def gram_kernel(row_count, vec_count, width, full_ref, gram_ref, hi_ref, lo_ref, own_ref, panel, inbox,
+                sum_send, sum_recv, deep_send, deep_recv, swap_send, swap_recv, over_send, over_recv,
+                side_send, side_recv):
+    row, vec = lax.axis_index("row"), lax.axis_index("vec")
+    rows, all_cols = full_ref.shape
+    chunks, span = all_cols // vec_count // width, width * vec_count
+    piece = panel.shape[0] // row_count
+    pairs, groups = row_count // 2, vec_count // 2
+    partner = row + 1 - 2 * (row % 2)
+    sibling = vec + 1 - 2 * (vec % 2)
+
+    barrier = pltpu.get_barrier_semaphore()
+    peers = [((row + d) % row_count, vec) for d in range(1, row_count)]
+    peers += [(row, (vec + 2 * d) % vec_count) for d in range(1, groups)] + [(row, sibling)]
+    for peer in peers:
+        pl.semaphore_signal(barrier, inc=1, device_id=peer, device_id_type=MESH)
+
+    step = 128
+
+    @pl.loop(0, rows // step)
+    def _(b):
+        at = pl.ds(pl.multiple_of(b * step, step), step)
+        hi, lo = split(full_ref[at, :])
+        hi_ref[at, :] = hi
+        lo_ref[at, :] = lo
+        for c in range(chunks):
+            mine = full_ref[at, pl.ds(pl.multiple_of(c * span + vec * width, width), width)].T
+            hi, lo = split(mine)
+            own_ref[c, pl.ds(0, width), at] = hi
+            own_ref[c, pl.ds(width, width), at] = lo
+
+    def give(d):
+        target = (row + d) % row_count
+        return pltpu.make_async_remote_copy(
+            panel.at[pl.ds(pl.multiple_of(target * piece, piece), piece)], inbox.at[d - 1],
+            sum_send.at[d - 1], sum_recv.at[d - 1], device_id=(target, vec), device_id_type=MESH)
+
+    tile = min(256, all_cols)
+    for c in range(chunks):
+        @pl.loop(0, all_cols // tile)
+        def _(t):
+            at = pl.ds(pl.multiple_of(t * tile, tile), tile)
+            both = dot(own_ref[c], hi_ref[:, at])
+            panel[pl.ds(c * width, width), at] = (
+                both[:width] + both[width:] + dot(own_ref[c, pl.ds(0, width), :], lo_ref[:, at])
+            )
+    pl.semaphore_wait(barrier, len(peers))
+    for d in range(1, row_count):
+        give(d).start()
+
+    def rows_of(r, v):
+        local = r * piece
+        return pl.ds(pl.multiple_of(local // width * span + v * width + local % width, piece), piece)
+
+    def send(r, v, sems, index, to):
+        at = gram_ref.at[rows_of(r, v)]
+        return pltpu.make_async_remote_copy(
+            at, at, sems[0].at[index], sems[1].at[index], device_id=to, device_id_type=MESH)
+
+    def row_of(k, base):
+        return (base + 2 * k) % row_count
+
+    def deep(d):
+        return send(row, vec, (deep_send, deep_recv), d - 1, (row_of(d, row), vec))
+
+    def swap(k):
+        return send(row_of(k, row), vec, (swap_send, swap_recv), k, (partner, vec))
+
+    def held(k):
+        return row_of(k, row) if k < pairs else row_of(k - pairs, partner)
+
+    def over(k, d):
+        return send(held(k), vec, (over_send, over_recv), (k, d - 1), (row, (vec + 2 * d) % vec_count))
+
+    def side(k, d):
+        return send(held(k), (vec + 2 * d) % vec_count, (side_send, side_recv), (k, d), (row, sibling))
+
+    acc = panel[pl.ds(pl.multiple_of(row * piece, piece), piece), :]
+    for d in range(1, row_count):
+        give(d).wait_recv()
+        acc = acc + inbox[d - 1]
+    gram_ref[rows_of(row, vec), :] = acc
+    for d in range(1, pairs):
+        deep(d).start()
+
+    def spread(k):
+        for d in range(1, groups):
+            over(k, d).start()
+        side(k, 0).start()
+
+    swap(0).start()
+    spread(0)
+    for d in range(1, pairs):
+        deep(pairs - d).wait_recv()
+        swap(d).start()
+        spread(d)
+    for k in range(pairs):
+        swap(k).wait_recv()
+        spread(pairs + k)
+    for k in range(row_count):
+        for d in range(1, groups):
+            over(k, groups - d).wait_recv()
+            side(k, d).start()
+    for d in range(1, row_count):
+        give(d).wait_send()
+    for d in range(1, pairs):
+        deep(d).wait_send()
+    for k in range(pairs):
+        swap(k).wait_send()
+    for k in range(row_count):
+        for d in range(1, groups):
+            over(k, d).wait_send()
+        for d in range(groups):
+            side(k, d).wait()
+
+
+def full_gram(row_count, vec_count, width, full):
+    rows, all_cols = full.shape
+    cols = all_cols // vec_count
+    vmem = pl.BlockSpec(memory_space=pltpu.VMEM)
+    dma = pltpu.SemaphoreType.DMA
+    pairs, groups = row_count // 2, vec_count // 2
+    others = max(1, groups - 1)
+    return pl.pallas_call(
+        functools.partial(gram_kernel, row_count, vec_count, width),
+        out_shape=jax.ShapeDtypeStruct((all_cols, all_cols), jnp.float32),
+        in_specs=[vmem],
+        out_specs=vmem,
+        scratch_shapes=[
+            pltpu.VMEM((rows, all_cols), jnp.bfloat16),
+            pltpu.VMEM((rows, all_cols), jnp.bfloat16),
+            pltpu.VMEM((cols // width, 2 * width, rows), jnp.bfloat16),
+            pltpu.VMEM((cols, all_cols), jnp.float32),
+            pltpu.VMEM((row_count - 1, cols // row_count, all_cols), jnp.float32),
+            dma((row_count - 1,)), dma((row_count - 1,)),
+            dma((max(1, pairs - 1),)), dma((max(1, pairs - 1),)),
+            dma((pairs,)), dma((pairs,)),
+            dma((row_count, others)), dma((row_count, others)),
+            dma((row_count, groups)), dma((row_count, groups)),
+        ],
+        compiler_params=pltpu.CompilerParams(
+            collective_id=1, has_side_effects=True, vmem_limit_bytes=50 * 1024 * 1024
+        ),
+    )(full)
+
+
 def on_device(vectors, hamiltonian, column_blocks, live_counts, lower_bound, upper_bound):
     rows_dev, panel_cols = vectors.shape
     block_rows = hamiltonian.shape[0]
@@ -215,18 +361,11 @@
 
     high = lax.Precision.HIGH
     span = width * vec_count
-    own = jnp.concatenate([
-        lax.dynamic_slice_in_dim(full_rows, c * span + lax.axis_index("vec") * width, width, axis=1)
+    gram = full_gram(row_count, vec_count, width, full_rows)
+    panel = jnp.concatenate([
+        lax.dynamic_slice_in_dim(gram, c * span + lax.axis_index("vec") * width, width, axis=1)
         for c in range(panel_cols // width)
     ], axis=1)
-    panel = lax.dot_general(
-        full_rows, own, (((0,), (0,)), ((), ())), precision=high, preferred_element_type=jnp.float32
-    )
-    panel = lax.psum(panel, "row")
-    panels = lax.all_gather(panel, "vec")
-    gram = jnp.concatenate(
-        [panels[v][:, c:c + width] for c in range(0, panel_cols, width) for v in range(vec_count)], axis=1
-    )
     energy = jnp.trace(gram)
     scale2 = all_cols / (4 * (energy + 1e-06))
     gram = gram * scale2

time: 350 us -> 275 us (0.79)
  waiting for transfers between devices: 117 us -> 0 us
  Pallas kernels: 153 us -> 230 us
  between operations: 15.7 us -> 2.18 us
  local copies, waits for them, and re-layouts: 12.6 us -> 1.29 us
  matrix products: 44.8 us -> 34.6 us
    psum x1 -> x0, waiting for transfers between devices: 80.5 us -> none  [on_device(): panel = lax.psum(panel, 'row')]
    pallas_call x0 -> x1, Pallas kernels: none -> 77.6 us  [full_gram(): pl.pallas_call(functools.partial(gram_kernel, row_count, vec_count, width...]
    all_gather x1 -> x0, waiting for transfers between devices: 36.6 us -> none  [on_device(): panels = lax.all_gather(panel, 'vec')]
    dot_general x1 -> x0, matrix products: 10.2 us -> none  [on_device(): lax.dot_general(full_rows, own, (((0,), (0,)), ((), ())), precision=high,...]
    unnamed x13 -> x2, local copies, waits for them, and re-layouts: 9.77 us -> 0.01 us
  transfers between devices with their start and end apart: 2 -> 0, of which waited for: 2 -> 0; matrix products, arithmetic and copies ran while one was open for 0% -> 0% of each run, Pallas kernels for 0% -> 0%
where the time goes in v3:
time: 275 us
  Pallas kernels  230 us (84%)
  matrix products  34.6 us (13%)
  other arithmetic  6.17 us (2%)
    pallas_call x1, Pallas kernels, filtered_rows(): pl.pallas_call(functools.partial(filter_kernel, row_count, vec_count, wid...  153 us
    pallas_call x1, Pallas kernels, full_gram(): pl.pallas_call(functools.partial(gram_kernel, row_count, vec_count, width...  77.6 us
    dot_general x12, matrix products, times_gram(): return jnp.dot(gram, x, precision=high)  27.4 us
    dot_general x1, matrix products, on_device(): return jnp.dot(full_rows, poly, precision=high)  7.17 us

profile of v3, /device:TPU:23, one launch (start us, length us, event | category | flops | bytes accessed | tf_op | source)
XLA Modules:
  0.0 274.7 jit_solution(13678773179756709520)
XLA Ops:
  0.0 1.3 fusion.44.pos_ref
  2.6 0.6 pad_maximum_fusion.coef_ref
  3.2 1.3 fusion.46.live_ref
  4.5 152.8 %shard_map.64.full_ref = f32[2048,1024]{1,0:T(8,128)} custom-call(s32[16,12]{1,0:T(8,128)} %fusion.44.pos_ref, f32[16,12]{1,0:T(8,128)} %fusion.46.live_ref, f32[2]{0:T(128)} %pad_maximum_fusion.coef_ref, f32[2048,256]{1,0:T(8,128)} %vec_ref.1, f32[16,12,128,128]{3,2,1,0:T(8,128)} %ham_ref.1), custom_call_target="tpu_custom_call" | custom-call | tf_op jit(solution)/shard_map/pallas_call | solution.py:167
  157.4 77.6 %shard_map.65 = f32[1024,1024]{1,0:T(8,128)} custom-call(f32[2048,1024]{1,0:T(8,128)} %shard_map.64.full_ref), custom_call_target="tpu_custom_call" | custom-call | tf_op jit(solution)/shard_map/pallas_call | solution.py:316
  235.0 1.3 constant_dynamic-slice_fusion.1
  236.2 2.9 %select_reduce_fusion = f32[]{:T(128)} fusion(f32[1024,1024]{1,0:T(8,128)} %shard_map.65), kind=kLoop, calls=%fused_computation | loop fusion | flops 3145727 | bytes 4194308 | tf_op jit(solution)/shard_map/jit(trace)/reduce_sum | solution.py:369
  239.9 0.0 copy-start
  239.9 4.4 %fusion.13 = f32[1024,256]{1,0:T(8,128)S(1)} fusion(f32[1024,1024]{1,0:T(8,128)} %shard_map.65, f32[]{:T(128)S(6)} %div.37, f32[1024,128]{1,0:T(8,128)S(1)} %get-tuple-element.6, f32[1024,128]{1,0:T(8,128)S(1)} %get-tuple-element.5, f32[]{:T(128)S(6)} %mul.118, s32[256]{0:T(256)S(1)} %fusion.49), kind=kOutput, calls=%fused_computation.16 | convolution fusion | flops 1615069184 | bytes 6292488 | tf_op jit(solution)/shard_map/dot_general | solution.py:378
  244.3 0.0 copy-done
  244.3 1.9 fusion.15
  246.2 1.9 fusion.17
  248.1 1.8 fusion.19
  250.0 1.9 fusion.21
  251.8 1.9 fusion.23
  253.7 2.1 fusion.25
  255.8 1.9 fusion.27
  257.7 1.9 fusion.29
  259.6 1.9 fusion.31
  261.5 1.9 fusion.33
  263.4 4.1 %fusion.36 = f32[1024,256]{1,0:T(8,128)S(1)} fusion(f32[1024,256]{1,0:T(8,128)S(1)} %fusion.33, f32[1024,1024]{1,0:T(8,128)} %shard_map.65, f32[]{:T(128)S(6)} %div.37, f32[1024,256]{1,0:T(8,128)S(1)} %fusion.17, f32[]{:T(128)S(6)} %mul.143), kind=kOutput, calls=%fused_computation.39 | convolution fusion | flops 1612709888 | bytes 7340040 | tf_op jit(solution)/shard_map/dot_general | solution.py:378
  267.5 7.2 %fusion.55 = f32[2048,256]{1,0:T(8,128)} fusion(f32[2048,1024]{1,0:T(8,128)} %shard_map.64.full_ref, f32[1024,256]{1,0:T(8,128)S(1)} %fusion.36), kind=kOutput, calls=%fused_computation.77 | convolution fusion | flops 3221225472 | bytes 11534336 | tf_op jit(solution)/shard_map/dot_general | solution.py:388
  (1 shorter events, 0.0 us)
Async XLA Ops:
  239.9 4.4 %copy-start = (f32[1024,1024]{1,0:T(8,128)S(1)}, f32[1024,1024]{1,0:T(8,128)}, u32[]{:S(2)}) copy-start(f32[1024,1024]{1,0:T(8,128)} %shard_map.65) | copy-start | bytes 12582916

commit v4 on v3

--- a/solution.py
+++ b/solution.py
@@ -102,24 +102,33 @@
             hi_ref[to] = hi
             lo_ref[to] = lo
 
-    for stage in range(2):
-        for c in range(chunks):
-            wide = pl.ds(c * width, width)
-
-            def own(at):
-                return first[c, at, :] if stage else vec_ref[at, wide]
-
-            for q in range(PIECES):
-                spread(own, 0, q)
-            for q in range(PIECES):
-                swap(stage, c, q).wait_recv()
-                pass_on(stage, c, q).start()
-                spread(lambda at: near[stage, c, at, :], 1, q)
-            for q in range(PIECES):
-                pass_on(stage, c, q).wait_recv()
-                spread(lambda at: far[stage, c, at, :], 2, q)
-
-            @pl.loop(0, block_rows)
+    def forward(stage, c, q):
+        swap(stage, c, q).wait_recv()
+        pass_on(stage, c, q).start()
+
+    def relay_all(c, q):
+        for d in range(len(overs)):
+            over(c, q, d).wait_recv()
+            relay(c, q, d).start()
+
+    order = [(stage, c) for stage in range(2) for c in range(chunks)]
+    for q in range(PIECES):
+        forward(0, 0, q)
+    for turn, (stage, c) in enumerate(order):
+        wide = pl.ds(c * width, width)
+
+        def own(at):
+            return first[c, at, :] if stage else vec_ref[at, wide]
+
+        for q in range(PIECES):
+            spread(own, 0, q)
+            spread(lambda at: near[stage, c, at, :], 1, q)
+        for q in range(PIECES):
+            pass_on(stage, c, q).wait_recv()
+            spread(lambda at: far[stage, c, at, :], 2, q)
+
+        for q in range(PIECES):
+            @pl.loop(q * block_rows // PIECES, (q + 1) * block_rows // PIECES)
             def _(i):
                 total = jnp.zeros((size, width), jnp.float32)
                 for k in range(0, slots, 2):
@@ -134,18 +143,20 @@
                 else:
                     first[c, at, :] = out
 
-            for q in range(PIECES):
-                if stage:
-                    for d in range(len(overs)):
-                        over(c, q, d).start()
-                    side(c, q).start()
-                else:
-                    swap(1, c, q).start()
+            if stage:
+                for d in range(len(overs)):
+                    over(c, q, d).start()
+                side(c, q).start()
+            else:
+                swap(1, c, q).start()
+            if turn + 1 < len(order):
+                forward(*order[turn + 1], q)
+            elif chunks > 1:
+                relay_all(0, q)
 
     for c, q in every:
-        for d in range(len(overs)):
-            over(c, q, d).wait_recv()
-            relay(c, q, d).start()
+        if c > 0 or chunks == 1:
+            relay_all(c, q)
     for c, q in every:
         side(c, q).wait()
         for d in range(len(overs)):

time: 275 us -> 258 us (0.938)
  Pallas kernels: 230 us -> 214 us
    pallas_call x1, Pallas kernels: 153 us -> 135 us  [filtered_rows(): pl.pallas_call(functools.partial(filter_kernel, row_count, vec_count, wid...]
where the time goes in v4:
time: 258 us
  Pallas kernels  214 us (83%)
  matrix products  34.6 us (13%)
  other arithmetic  6.17 us (2%)
    pallas_call x1, Pallas kernels, filtered_rows(): pl.pallas_call(functools.partial(filter_kernel, row_count, vec_count, wid...  135 us
    pallas_call x1, Pallas kernels, full_gram(): pl.pallas_call(functools.partial(gram_kernel, row_count, vec_count, width...  78.8 us
    dot_general x12, matrix products, times_gram(): return jnp.dot(gram, x, precision=high)  27.5 us
    dot_general x1, matrix products, on_device(): return jnp.dot(full_rows, poly, precision=high)  7.17 us

profile of v4, /device:TPU:23, one launch (start us, length us, event | category | flops | bytes accessed | tf_op | source)
XLA Modules:
  0.0 258.0 jit_solution(11931190691883375504)
XLA Ops:
  0.0 1.3 fusion.44.pos_ref
  2.6 0.6 pad_maximum_fusion.coef_ref
  3.2 1.3 fusion.46.live_ref
  4.5 135.0 %shard_map.64.full_ref = f32[2048,1024]{1,0:T(8,128)} custom-call(s32[16,12]{1,0:T(8,128)} %fusion.44.pos_ref, f32[16,12]{1,0:T(8,128)} %fusion.46.live_ref, f32[2]{0:T(128)} %pad_maximum_fusion.coef_ref, f32[2048,256]{1,0:T(8,128)} %vec_ref.1, f32[16,12,128,128]{3,2,1,0:T(8,128)} %ham_ref.1), custom_call_target="tpu_custom_call" | custom-call | tf_op jit(solution)/shard_map/pallas_call | solution.py:178
  139.5 78.8 %shard_map.65 = f32[1024,1024]{1,0:T(8,128)} custom-call(f32[2048,1024]{1,0:T(8,128)} %shard_map.64.full_ref), custom_call_target="tpu_custom_call" | custom-call | tf_op jit(solution)/shard_map/pallas_call | solution.py:327
  218.3 1.3 constant_dynamic-slice_fusion.1
  219.6 2.9 %select_reduce_fusion = f32[]{:T(128)} fusion(f32[1024,1024]{1,0:T(8,128)} %shard_map.65), kind=kLoop, calls=%fused_computation | loop fusion | flops 3145727 | bytes 4194308 | tf_op jit(solution)/shard_map/jit(trace)/reduce_sum | solution.py:380
  223.2 0.0 copy-start
  223.2 4.4 %fusion.13 = f32[1024,256]{1,0:T(8,128)S(1)} fusion(f32[1024,1024]{1,0:T(8,128)} %shard_map.65, f32[]{:T(128)S(6)} %div.37, f32[1024,128]{1,0:T(8,128)S(1)} %get-tuple-element.6, f32[1024,128]{1,0:T(8,128)S(1)} %get-tuple-element.5, f32[]{:T(128)S(6)} %mul.118, s32[256]{0:T(256)S(1)} %fusion.49), kind=kOutput, calls=%fused_computation.16 | convolution fusion | flops 1615069184 | bytes 6292488 | tf_op jit(solution)/shard_map/dot_general | solution.py:389
  227.6 0.0 copy-done
  227.7 1.9 fusion.15
  229.5 1.9 fusion.17
  231.5 1.8 fusion.19
  233.3 1.9 fusion.21
  235.2 1.9 fusion.23
  237.1 2.1 fusion.25
  239.2 1.9 fusion.27
  241.1 1.9 fusion.29
  243.0 1.9 fusion.31
  244.9 1.9 fusion.33
  246.8 4.1 %fusion.36 = f32[1024,256]{1,0:T(8,128)S(1)} fusion(f32[1024,256]{1,0:T(8,128)S(1)} %fusion.33, f32[1024,1024]{1,0:T(8,128)} %shard_map.65, f32[]{:T(128)S(6)} %div.37, f32[1024,256]{1,0:T(8,128)S(1)} %fusion.17, f32[]{:T(128)S(6)} %mul.143), kind=kOutput, calls=%fused_computation.39 | convolution fusion | flops 1612709888 | bytes 7340040 | tf_op jit(solution)/shard_map/dot_general | solution.py:389
  250.9 7.2 %fusion.55 = f32[2048,256]{1,0:T(8,128)} fusion(f32[2048,1024]{1,0:T(8,128)} %shard_map.64.full_ref, f32[1024,256]{1,0:T(8,128)S(1)} %fusion.36), kind=kOutput, calls=%fused_computation.77 | convolution fusion | flops 3221225472 | bytes 11534336 | tf_op jit(solution)/shard_map/dot_general | solution.py:399
  (1 shorter events, 0.0 us)
Async XLA Ops:
  223.2 4.4 %copy-start = (f32[1024,1024]{1,0:T(8,128)S(1)}, f32[1024,1024]{1,0:T(8,128)}, u32[]{:S(2)}) copy-start(f32[1024,1024]{1,0:T(8,128)} %shard_map.65) | copy-start | bytes 12582916

commit v5 on v4

--- a/solution.py
+++ b/solution.py
@@ -80,7 +80,7 @@
         return across(c, q, sources[d], relay_send.at[c, q, d], relay_recv.at[c, q, d], sibling)
 
     every = [(c, q) for c in range(chunks) for q in range(PIECES)]
-    for c, q in every:
+    for c, q in every[:3]:
         swap(0, c, q).start()
 
     copy.wait()
@@ -105,6 +105,9 @@
     def forward(stage, c, q):
         swap(stage, c, q).wait_recv()
         pass_on(stage, c, q).start()
+        later = c * PIECES + q + 3
+        if stage == 0 and later < len(every):
+            swap(0, *every[later]).start()
 
     def relay_all(c, q):
         for d in range(len(overs)):
@@ -347,13 +350,87 @@
     )(full)
 
 
+def finish_kernel(total_rows, span, width, vec_ref, full_ref, gram_ref, out_ref, ghi, glo, xhi, xlo, *bufs):
+    vec = vec_ref[0]
+    rows, all_cols = full_ref.shape
+    cols = out_ref.shape[1]
+    step = 128
+    diagonal = (
+        lax.broadcasted_iota(jnp.int32, (step, step), 0) == lax.broadcasted_iota(jnp.int32, (step, step), 1)
+    ).astype(jnp.float32)
+    energy = jnp.zeros((step, step), jnp.float32)
+    for b in range(0, all_cols, step):
+        energy += gram_ref[pl.ds(b, step), pl.ds(b, step)] * diagonal
+    energy = jnp.sum(jnp.sum(energy, axis=1, keepdims=True), axis=0, keepdims=True)
+    scale2 = all_cols / (4 * (energy + 1e-06))
+    poly, spare = bufs[:2]
+
+    @pl.loop(0, all_cols // step)
+    def _(b):
+        at = pl.ds(pl.multiple_of(b * step, step), step)
+        ghi[at, :], glo[at, :] = split(gram_ref[at, :] * scale2)
+        for c in range(cols // width):
+            first_col = pl.multiple_of(c * span + vec * width, width)
+            row_ids = b * step + lax.broadcasted_iota(jnp.int32, (step, width), 0)
+            col_ids = first_col + lax.broadcasted_iota(jnp.int32, (step, width), 1)
+            eye = (row_ids == col_ids).astype(jnp.float32)
+            poly[at, pl.ds(c * width, width)] = 1.5 * eye - 0.5 * (gram_ref[at, pl.ds(first_col, width)] * scale2)
+
+    tile = 256
+
+    def three(hi, lo):
+        return dot(hi, xhi[...]) + dot(lo, xhi[...]) + dot(hi, xlo[...])
+
+    def times_gram(level, dst, src, base):
+        if level == 0:
+            xhi[...], xlo[...] = split(src[...])
+
+            @pl.loop(0, all_cols // tile)
+            def _(t):
+                at = pl.ds(pl.multiple_of(t * tile, tile), tile)
+                out = three(ghi[at, :], glo[at, :])
+                dst[at, :] = out if base is None else 1.5 * base[at, :] - 0.5 * out
+            return
+        one, two = bufs[2 * level], bufs[2 * level + 1]
+        times_step(level - 1, one, src)
+        times_step(level - 1, two, one)
+        times_gram(level - 1, dst, two, base)
+
+    def times_step(level, dst, src):
+        times_gram(level, dst, src, src)
+
+    for level in range(1, NS_ITERS):
+        times_step(level, spare, poly)
+        poly, spare = spare, poly
+    xhi[...], xlo[...] = split(poly[...] * (jnp.sqrt(scale2) * math.sqrt(total_rows)))
+
+    @pl.loop(0, rows // tile)
+    def _(t):
+        at = pl.ds(pl.multiple_of(t * tile, tile), tile)
+        out_ref[at, :] = three(*split(full_ref[at, :]))
+
+
+def finish(total_rows, span, width, vec, cols, full, gram):
+    rows, all_cols = full.shape
+    vmem = pl.BlockSpec(memory_space=pltpu.VMEM)
+    return pl.pallas_call(
+        functools.partial(finish_kernel, total_rows, span, width),
+        out_shape=jax.ShapeDtypeStruct((rows, cols), jnp.float32),
+        in_specs=[pl.BlockSpec(memory_space=pltpu.SMEM), vmem, vmem],
+        out_specs=vmem,
+        scratch_shapes=[pltpu.VMEM((all_cols, all_cols), jnp.bfloat16)] * 2
+        + [pltpu.VMEM((all_cols, cols), jnp.bfloat16)] * 2
+        + [pltpu.VMEM((all_cols, cols), jnp.float32)] * (2 * NS_ITERS),
+        compiler_params=pltpu.CompilerParams(vmem_limit_bytes=50 * 1024 * 1024),
+    )(vec, full, gram)
+
+
 def on_device(vectors, hamiltonian, column_blocks, live_counts, lower_bound, upper_bound):
     rows_dev, panel_cols = vectors.shape
     block_rows = hamiltonian.shape[0]
     row_count = lax.axis_size("row")
     vec_count = lax.axis_size("vec")
     me = lax.axis_index("row")
-    all_cols = panel_cols * vec_count
 
     rel = (column_blocks - me * block_rows + block_rows) % (block_rows * row_count)
     side = rel // block_rows
@@ -370,33 +447,10 @@
         row_count, vec_count, width, pos, live, coef, vectors, hamiltonian
     )
 
-    high = lax.Precision.HIGH
     span = width * vec_count
     gram = full_gram(row_count, vec_count, width, full_rows)
-    panel = jnp.concatenate([
-        lax.dynamic_slice_in_dim(gram, c * span + lax.axis_index("vec") * width, width, axis=1)
-        for c in range(panel_cols // width)
-    ], axis=1)
-    energy = jnp.trace(gram)
-    scale2 = all_cols / (4 * (energy + 1e-06))
-    gram = gram * scale2
-    local = jnp.arange(panel_cols)
-    column = local // width * (width * vec_count) + lax.axis_index("vec") * width + local % width
-    eye = (jnp.arange(all_cols)[:, None] == column[None, :]).astype(jnp.float32)
-
-    def times_gram(level, x):
-        if level == 0:
-            return jnp.dot(gram, x, precision=high)
-        return times_gram(level - 1, times_step(level - 1, times_step(level - 1, x)))
-
-    def times_step(level, x):
-        return 1.5 * x - 0.5 * times_gram(level, x)
-
-    poly = 1.5 * eye - 0.5 * panel * scale2
-    for level in range(1, NS_ITERS):
-        poly = times_step(level, poly)
-    poly = poly * (jnp.sqrt(scale2) * math.sqrt(rows_dev * row_count))
-    return jnp.dot(full_rows, poly, precision=high)
+    vec = jnp.full((1,), lax.axis_index("vec"), jnp.int32)
+    return finish(rows_dev * row_count, span, width, vec, panel_cols, full_rows, gram)
 
 
 def solution(mesh):

time: 258 us -> 263 us (1.019)
  Pallas kernels: 214 us -> 258 us
  matrix products: 34.6 us -> 0 us
  other arithmetic: 6.17 us -> 3.23 us
    pallas_call x0 -> x1, Pallas kernels: none -> 41.4 us  [finish(): pl.pallas_call(functools.partial(finish_kernel, total_rows, span, width),...]
    dot_general x13 -> x0, matrix products: 34.6 us -> none  [the longest x12 27.5 us: times_gram(): return jnp.dot(gram, x, precision=high)]
    reduce_sum x1 -> x0, other arithmetic: 2.93 us -> none  [on_device(): energy = jnp.trace(gram)]
where the time goes in v5:
time: 263 us; the launch traced here: 262 us
  Pallas kernels  258 us (98%)
  other arithmetic  3.23 us (1%)
    pallas_call x1, Pallas kernels, filtered_rows(): pl.pallas_call(functools.partial(filter_kernel, row_count, vec_count, wid...  137 us
    pallas_call x1, Pallas kernels, full_gram(): pl.pallas_call(functools.partial(gram_kernel, row_count, vec_count, width...  79.6 us
    pallas_call x1, Pallas kernels, finish(): pl.pallas_call(functools.partial(finish_kernel, total_rows, span, width),...  41.4 us

profile of v5, /device:TPU:23, one launch (start us, length us, event | category | flops | bytes accessed | tf_op | source)
XLA Modules:
  0.0 262.4 jit_solution(8621178647742694714)
XLA Ops:
  1.3 0.6 pad_maximum_fusion.coef_ref
  1.9 1.3 fusion.1.pos_ref
  3.2 1.3 fusion.3.live_ref
  4.5 136.9 %shard_map.64.full_ref = f32[2048,1024]{1,0:T(8,128)} custom-call(s32[16,12]{1,0:T(8,128)} %fusion.1.pos_ref, f32[16,12]{1,0:T(8,128)} %fusion.3.live_ref, f32[2]{0:T(128)} %pad_maximum_fusion.coef_ref, f32[2048,256]{1,0:T(8,128)} %vec_ref.1, f32[16,12,128,128]{3,2,1,0:T(8,128)} %ham_ref.1), custom_call_target="tpu_custom_call" | custom-call | tf_op jit(solution)/shard_map/pallas_call | solution.py:181
  141.4 79.6 %shard_map.65.gram_ref = f32[1024,1024]{1,0:T(8,128)} custom-call(f32[2048,1024]{1,0:T(8,128)} %shard_map.64.full_ref), custom_call_target="tpu_custom_call" | custom-call | tf_op jit(solution)/shard_map/pallas_call | solution.py:330
  221.0 41.4 %shard_map.66 = f32[2048,256]{1,0:T(8,128)} custom-call(s32[1]{0:T(128)} %bitcast.vec_ref, f32[2048,1024]{1,0:T(8,128)} %shard_map.64.full_ref, f32[1024,1024]{1,0:T(8,128)} %shard_map.65.gram_ref), custom_call_target="tpu_custom_call" | custom-call | tf_op jit(solution)/shard_map/pallas_call | solution.py:416
